TPU v7x, 256 devices: a whole 4x4x8 slice. The times are simulated.
256 devices in a mesh: tensor: 4 (over y_lo, core), context: 64 (over y_hi, x, z).
Axes of the slice: x: 4, y: 4 (y_hi: 2, y_lo: 2; y = y_hi * 2 + y_lo), z: 8, core: 2. Of those that a mesh axis runs over, the one named last changes fastest.
Arguments:
- hidden_in: bfloat16 [64, 128, 4096], P('context'), may hold values from -12 to 12
- value_first: bfloat16 [64, 128, 512], P('context', None, 'tensor'), may hold values from -6 to 6
- w_query: bfloat16 [4096, 2048], P(None, 'tensor'), may hold values from -0.09375 to 0.09375
- w_key: bfloat16 [4096, 512], P(None, 'tensor'), may hold values from -0.09375 to 0.09375
- w_value: bfloat16 [4096, 512], P(None, 'tensor'), may hold values from -0.09375 to 0.09375
- w_out: bfloat16 [2048, 4096], P('tensor'), may hold values from -0.125 to 0.125
- value_mix: float32 [2, 4], P(None, 'tensor'), may hold values from 0.2 to 1
- grad_out: bfloat16 [64, 128, 4096], P('context', 'tensor'), may hold values from -3 to 3
Outputs:
- attn_out: bfloat16 [64, 128, 4096], P('context', 'tensor')
- grad_in: bfloat16 [64, 128, 4096], P('context', 'tensor')
- grad_value_first: bfloat16 [64, 128, 512], P('context', None, 'tensor')
- grad_w_key: float32 [4096, 512], P('context', 'tensor')
- grad_w_value: float32 [4096, 512], P('context', 'tensor')
All inputs are finite; a program needn't handle non-finite values.
Results may differ from a plain program's by a relative error of at most 0.03.
The roundings to bfloat16 on the way count: a program that leaves them out, or rounds other values in their place, can miss the bound.
Values may be sent and summed in bfloat16 or wider, within the bound.
A program may use at most 128 MiB of HBM per device.

v0:
```python
import jax
import jax.numpy as jnp
from jax import lax
from jax.sharding import PartitionSpec as P

HD = 128


THETA = 500000.0
NEGATIVE = -1e30


def rope_tables(positions, head_width):
    half_width = head_width // 2
    exponent = jnp.arange(half_width, dtype=jnp.float32) * (2.0 / head_width)
    frequency = jnp.power(jnp.float32(THETA), -exponent)
    angles = positions.astype(jnp.float32)[:, None] * frequency[None, :]
    return (jnp.cos(angles), jnp.sin(angles))


def rotate(field, cosine_table, sine_table):
    half_width = field.shape[-1] // 2
    first_half = field[..., :half_width]
    second_half = field[..., half_width:]
    cosine_part = cosine_table[:, None, :]
    sine_part = sine_table[:, None, :]
    return jnp.concatenate(
        [
            first_half * cosine_part - second_half * sine_part,
            second_half * cosine_part + first_half * sine_part,
        ],
        axis=-1,
    )


def times_transpose(left_side, right_side):
    return lax.dot_general(
        left_side, right_side, (((1,), (1,)), ((), ())), preferred_element_type=jnp.float32
    )


def unchanged(current):
    return current


def shards(hidden_in, value_first, w_query, w_key, w_value, w_out, value_mix, grad_out):
    tensor_count = lax.axis_size("tensor")
    context_count = lax.axis_size("context")
    context_rank = lax.axis_index("context")
    model_width = hidden_in.shape[2]
    head_width = HD
    local_kv = w_key.shape[1] // head_width
    local_heads = w_query.shape[1] // head_width
    group_size = local_heads // local_kv
    kv_width = local_kv * head_width
    length = hidden_in.shape[1]
    share_rows = length // tensor_count
    score_scale = head_width ** (-0.5)
    inputs = hidden_in.reshape(length, model_width)
    firsts = value_first.reshape(length, kv_width)
    block_rows = context_rank * length + jnp.arange(length, dtype=jnp.int32)
    cosine_table, sine_table = rope_tables(block_rows, head_width)
    query_raw = jnp.dot(inputs, w_query, preferred_element_type=jnp.float32).reshape(
        length, local_heads, head_width
    )
    queries = (
        rotate(query_raw, cosine_table, sine_table)
        .astype(jnp.bfloat16)
        .reshape(length, local_heads * head_width)
    )
    key_raw = jnp.dot(inputs, w_key, preferred_element_type=jnp.float32).reshape(
        length, local_kv, head_width
    )
    key_rows = (
        rotate(key_raw, cosine_table, sine_table).astype(jnp.bfloat16).reshape(length, kv_width)
    )
    value_proj = jnp.dot(inputs, w_value, preferred_element_type=jnp.float32).reshape(
        length, local_kv, head_width
    )
    mixed = value_mix[0][None, :, None] * value_proj + value_mix[1][None, :, None] * firsts.reshape(
        length, local_kv, head_width
    ).astype(jnp.float32)
    mixed_values = mixed.astype(jnp.bfloat16).reshape(length, kv_width)
    queries_here, keys_here, values_here = (queries, key_rows, mixed_values)
    query_last = jnp.max(block_rows)
    query_four = queries_here.reshape(length, local_kv, group_size, head_width)
    visible_rows = block_rows[:, None]

    def over_blocks(block_fn, running, pieces):
        row_count = pieces[0].shape[0]
        block_count = row_count // length

        def step_block(current, block_items):
            offset = block_items[-1]
            return (block_fn(current, block_items[:-1], offset), None)

        block_items = tuple((piece.reshape(block_count, length, -1) for piece in pieces)) + (
            jnp.arange(block_count, dtype=jnp.int32) * length,
        )
        return lax.scan(step_block, running, block_items)[0]

    def block_scores(key_block, key_positions):
        key_count = key_block.shape[0]
        key_four = key_block.reshape(key_count, local_kv, head_width)
        scores = (
            jnp.einsum("qkgd,nkd->kgqn", query_four, key_four, preferred_element_type=jnp.float32)
            * score_scale
        )
        visible = key_positions[None, :] <= visible_rows
        return (jnp.where(visible, scores, NEGATIVE), visible)

    def stats_block(running, pieces, first_row):
        key_block = pieces[0]
        key_positions = first_row + jnp.arange(key_block.shape[0], dtype=jnp.int32)

        def stats_update(current):
            maxima, totals = current
            masked, visible = block_scores(key_block, key_positions)
            new_max = jnp.maximum(maxima, jnp.max(masked, axis=-1))
            weights = jnp.where(visible, jnp.exp(masked - new_max[..., None]), 0.0)
            return (new_max, totals * jnp.exp(maxima - new_max) + jnp.sum(weights, axis=-1))

        return lax.cond(jnp.min(key_positions) > query_last, unchanged, stats_update, running)

    stats_start = (
        jnp.full((local_kv, group_size, length), NEGATIVE, jnp.float32),
        jnp.zeros((local_kv, group_size, length), jnp.float32),
    )
    output_start = jnp.zeros((local_kv, group_size, length, head_width), jnp.float32)

    def output_block(running, pieces, first_row):
        key_block, value_block = pieces
        key_count = key_block.shape[0]
        key_positions = first_row + jnp.arange(key_count, dtype=jnp.int32)

        def output_update(accumulated):
            masked, visible = block_scores(key_block, key_positions)
            weights = jnp.where(visible, jnp.exp(masked - log_total[..., None]), 0.0).astype(
                jnp.bfloat16
            )
            value_four = value_block.reshape(key_count, local_kv, head_width)
            return accumulated + jnp.einsum(
                "kgqn,nkd->kgqd", weights, value_four, preferred_element_type=jnp.float32
            )

        return lax.cond(jnp.min(key_positions) > query_last, unchanged, output_update, running)

    maxima, totals = over_blocks(
        stats_block, stats_start, (lax.all_gather(keys_here, "context", axis=0, tiled=True),)
    )
    log_total = maxima + jnp.log(totals)
    accumulated = over_blocks(
        output_block,
        output_start,
        (
            lax.all_gather(keys_here, "context", axis=0, tiled=True),
            lax.all_gather(values_here, "context", axis=0, tiled=True),
        ),
    )
    outputs_here = accumulated.astype(jnp.bfloat16)
    outputs_flat = outputs_here.transpose(2, 0, 1, 3).reshape(length, local_heads * head_width)
    attn_out = lax.psum_scatter(
        jnp.dot(outputs_flat, w_out, preferred_element_type=jnp.float32).astype(jnp.bfloat16),
        "tensor",
        scatter_dimension=0,
        tiled=True,
    ).reshape(1, share_rows, model_width)
    grads = lax.all_gather(grad_out, "tensor", axis=1, tiled=True).reshape(length, model_width)
    dout_block = times_transpose(grads, w_out).astype(jnp.bfloat16)
    dout_four = dout_block.reshape(length, local_kv, group_size, head_width)
    row_delta = jnp.sum(
        dout_four.transpose(1, 2, 0, 3).astype(jnp.float32) * outputs_here.astype(jnp.float32),
        axis=-1,
    )
    keys_back, values_back = (
        lax.all_gather(keys_here, "context", axis=0, tiled=True),
        lax.all_gather(values_here, "context", axis=0, tiled=True),
    )

    def back_block(query_grad, block_items):
        key_block, value_block, offset = block_items
        key_positions = offset + jnp.arange(length, dtype=jnp.int32)

        def compute(grad_now):
            key_four = key_block.reshape(length, local_kv, head_width)
            value_four = value_block.reshape(length, local_kv, head_width)
            masked, visible = block_scores(key_block, key_positions)
            probabilities = jnp.where(visible, jnp.exp(masked - log_total[..., None]), 0.0)
            prob_grads = jnp.einsum(
                "qkgd,nkd->kgqn", dout_four, value_four, preferred_element_type=jnp.float32
            )
            score_grads = (probabilities * (prob_grads - row_delta[..., None])).astype(jnp.bfloat16)
            grad_next = grad_now + score_scale * jnp.einsum(
                "kgqn,nkd->kgqd", score_grads, key_four, preferred_element_type=jnp.float32
            )
            key_term = score_scale * jnp.einsum(
                "kgqn,qkgd->nkd", score_grads, query_four, preferred_element_type=jnp.float32
            )
            value_term = jnp.einsum(
                "kgqn,qkgd->nkd",
                probabilities.astype(jnp.bfloat16),
                dout_four,
                preferred_element_type=jnp.float32,
            )
            return (
                grad_next,
                jnp.concatenate(
                    [key_term.reshape(length, kv_width), value_term.reshape(length, kv_width)],
                    axis=1,
                ),
            )

        def skipped(grad_now):
            return (grad_now, jnp.zeros((length, 2 * kv_width), jnp.float32))

        return lax.cond(jnp.min(key_positions) > query_last, skipped, compute, query_grad)

    back_items = (
        keys_back.reshape(context_count, length, kv_width),
        values_back.reshape(context_count, length, kv_width),
        jnp.arange(context_count, dtype=jnp.int32) * length,
    )
    query_grad, key_terms = lax.scan(
        back_block, jnp.zeros((local_kv, group_size, length, head_width), jnp.float32), back_items
    )
    key_sums = lax.psum_scatter(
        key_terms.reshape(context_count * length, 2 * kv_width),
        "context",
        scatter_dimension=0,
        tiled=True,
    )
    cosine_here, sine_here = rope_tables(block_rows, head_width)
    query_pre = (
        rotate(
            query_grad.transpose(2, 0, 1, 3).reshape(length, local_heads, head_width),
            cosine_here,
            -sine_here,
        )
        .astype(jnp.bfloat16)
        .reshape(length, local_heads * head_width)
    )
    key_pre = (
        rotate(
            key_sums[:, :kv_width].reshape(length, local_kv, head_width), cosine_here, -sine_here
        )
        .astype(jnp.bfloat16)
        .reshape(length, kv_width)
    )
    value_sum = key_sums[:, kv_width:].reshape(length, local_kv, head_width)
    value_pre = (
        (value_mix[0][None, :, None] * value_sum).astype(jnp.bfloat16).reshape(length, kv_width)
    )
    first_grad = (
        (value_mix[1][None, :, None] * value_sum).astype(jnp.bfloat16).reshape(length, kv_width)
    )
    summed = times_transpose(query_pre, w_query)
    summed = summed + times_transpose(key_pre, w_key)
    grad_in = lax.psum_scatter(
        (summed + times_transpose(value_pre, w_value)).astype(jnp.bfloat16),
        "tensor",
        scatter_dimension=0,
        tiled=True,
    ).reshape(1, share_rows, model_width)
    first_back = first_grad.reshape(1, length, kv_width)
    key_value_pre = jnp.concatenate([key_pre, value_pre], axis=1)
    weight_sums = lax.psum_scatter(
        lax.dot_general(
            inputs, key_value_pre, (((0,), (0,)), ((), ())), preferred_element_type=jnp.float32
        ),
        "context",
        scatter_dimension=0,
        tiled=True,
    )
    return (attn_out, grad_in, first_back, weight_sums[:, :kv_width], weight_sums[:, kv_width:])


def solution(mesh):
    return jax.shard_map(
        shards,
        mesh=mesh,
        in_specs=(
            P("context", None, None),
            P("context", None, "tensor"),
            P(None, "tensor"),
            P(None, "tensor"),
            P(None, "tensor"),
            P("tensor", None),
            P(None, "tensor"),
            P("context", "tensor", None),
        ),
        out_specs=(
            P("context", "tensor", None),
            P("context", "tensor", None),
            P("context", None, "tensor"),
            P("context", "tensor"),
            P("context", "tensor"),
        ),
        check_vma=False,
    )
```

profile of v0, /device:TPU:32, one launch (start us, length us, event | category | flops | bytes accessed | tf_op | source)
XLA Modules:
  0.0 2242.1 jit_solution(9216682099982024060)
XLA Ops:
  15.1 6.3 copy.91
  25.1 10.6 all-gather.8.cloned.1.call-done
  39.9 100.3 %all-gather.4.cloned.1.call-done = bf16[8192,128]{0,1:T(8,128)(2,1)} async-done(((bf16[128,128]{0,1:T(8,128)(2,1)}), bf16[8192,128]{0,1:T(8,128)(2,1)}) %all-gather.4.cloned.1.call-update) | async-done | bytes 2097168 | tf_op jit(solution)/shard_map/all_gather | solution.py:156
  144.2 203.8 %while.43 = (s32[]{:T(128)}, f32[1,4,128]{2,1,0:T(4,128)S(1)}, f32[1,4,128]{2,1,0:T(4,128)S(1)}, s32[64]{0:T(128)S(1)}, s32[]{:T(128)}, /*index=5*/bf16[64,128,1...) while((s32[]{:T(128)}, f32[1,4,128]{2,1,0:T(4,128)S(1)}, ...), condition=%wide.region_7.8_spmd.clone, body=%wide.region_1.7_spmd.clone.sunk | while | flops 17188228 | bytes 767715 | solution.py:100
  352.2 201.0 %while.44 = (s32[]{:T(128)}, f32[1,4,128,128]{3,2,1,0:T(8,128)S(1)}, s32[64]{0:T(128)S(1)}, s32[]{:T(128)}, bf16[64,128,128]{2,1,0:T(8,128)(2,1)}, /*index=5*/bf...) while((s32[]{:T(128)}, ...), condition=%wide.region_12.13_spmd.clone, body=%wide.region_8.12_spmd.clone.sunk | while | flops 33964416 | bytes 760027 | solution.py:100
  553.4 505.7 %while.45 = (s32[]{:T(128)}, f32[1,4,128,128]{3,2,1,0:T(8,128)S(1)}, f32[64,128,256]{1,0,2:T(8,128)}, s32[64]{0:T(128)S(1)}, s32[]{:T(128)}, /*index=5*/bf16[64,...) while((s32[]{:T(128)}, ...), condition=%wide.region_19.20_spmd.clone, body=%wide.region_15.19_spmd.clone.sunk | while | flops 84607360 | bytes 3023639 | solution.py:223
  559.9 4.7 dynamic_update_slice.6
  571.2 4.7 dynamic_update_slice.6
  579.0 4.7 dynamic_update_slice.6
  586.8 4.7 dynamic_update_slice.6
  594.6 4.7 dynamic_update_slice.6
  602.4 4.7 dynamic_update_slice.6
  610.2 4.7 dynamic_update_slice.6
  618.0 4.7 dynamic_update_slice.6
  750.2 4.7 dynamic_update_slice.6
  758.1 4.7 dynamic_update_slice.6
  765.9 4.7 dynamic_update_slice.6
  773.7 4.7 dynamic_update_slice.6
  781.5 4.7 dynamic_update_slice.6
  789.4 4.7 dynamic_update_slice.6
  797.2 4.7 dynamic_update_slice.6
  805.0 4.7 dynamic_update_slice.6
  812.9 4.7 dynamic_update_slice.6
  820.7 4.7 dynamic_update_slice.6
  828.5 4.7 dynamic_update_slice.6
  836.3 4.7 dynamic_update_slice.6
  844.1 4.7 dynamic_update_slice.6
  851.9 4.7 dynamic_update_slice.6
  859.7 4.7 dynamic_update_slice.6
  867.5 4.7 dynamic_update_slice.6
  875.3 4.7 dynamic_update_slice.6
  883.1 4.7 dynamic_update_slice.6
  890.9 4.7 dynamic_update_slice.6
  898.7 4.7 dynamic_update_slice.6
  999.8 4.7 dynamic_update_slice.6
  1007.6 4.7 dynamic_update_slice.6
  1015.4 4.7 dynamic_update_slice.6
  1023.2 4.7 dynamic_update_slice.6
  1031.0 4.7 dynamic_update_slice.6
  1038.8 4.7 dynamic_update_slice.6
  1046.6 4.7 dynamic_update_slice.6
  1054.4 4.7 dynamic_update_slice.6
  1059.1 14.3 copy.104
  1073.5 736.9 %reduce-scatter.9.cloned.1.call-done = f32[128,256]{0,1:T(8,128)} async-done(((f32[8192,256]{0,1:T(8,128)}), f32[128,256]{0,1:T(8,128)}) %reduce-scatter.9.cloned.1.call-update) | async-done | bytes 131088 | tf_op jit(solution)/shard_map/reduce_scatter | solution.py:226
  1815.4 5.6 copy.92
  1831.8 352.5 %reduce-scatter.13.cloned.1.call-done = f32[64,256]{1,0:T(8,128)} async-done(((f32[4096,256]{1,0:T(8,128)}), f32[64,256]{1,0:T(8,128)}) %reduce-scatter.13.cloned.1.call-update) | async-done | bytes 65552
  2185.7 22.4 %reduce-scatter.7.cloned.1.call-done = bf16[32,4096]{1,0:T(8,128)(2,1)} async-done(((bf16[128,4096]{1,0:T(8,128)(2,1)}), bf16[32,4096]{1,0:T(8,128)(2,1)}) %reduce-scatter.7.cloned.1.call-update) | async-done | bytes 262160 | tf_op jit(solution)/shard_map/reduce_scatter | solution.py:162
  2208.2 27.0 %reduce-scatter.11.cloned.1.call-done = bf16[32,4096]{1,0:T(8,128)(2,1)} async-done(((bf16[128,4096]{1,0:T(8,128)(2,1)}), bf16[32,4096]{1,0:T(8,128)(2,1)}) %reduce-scatter.11.cloned.1.call-update) | async-done | bytes 262160 | tf_op jit(solution)/shard_map/reduce_scatter | solution.py:258
  (1082 shorter events, 561.4 us)
Async XLA Ops:
  7.2 1.2 copy-start
  7.2 3.9 copy-start.3
  7.2 4.0 copy-start.4
  7.2 4.6 copy-start.2
  7.2 28.5 %all-gather.8.cloned.1.call-start = ((), (), s32[]{:S(2)}) async-start(), calls=%async_computation.7 | async-start | bytes 1310720 | tf_op jit(solution)/shard_map/all_gather | solution.py:168
  7.9 132.2 %all-gather.4.cloned.1.call-start = ((), (), s32[]{:S(2)}) async-start(), calls=%async_computation.4 | async-start | bytes 2129920 | tf_op jit(solution)/shard_map/all_gather | solution.py:156
  11.0 337.1 %all-gather.6.cloned.1.call-start = ((), (), s32[]{:S(2)}) async-start(), calls=%async_computation.5 | async-start | bytes 2129920 | tf_op jit(solution)/shard_map/all_gather | solution.py:157
  14.2 1796.1 %reduce-scatter.9.cloned.1.call-start = ((), (), s32[]{:S(2)}) async-start(), calls=%async_computation.8 | async-start | bytes 8519680 | tf_op jit(solution)/shard_map/reduce_scatter | solution.py:226
  1073.4 1110.9 %reduce-scatter.13.cloned.1.call-start = ((), (), s32[]{:S(2)}) async-start(), calls=%async_computation.10 | async-start | bytes 4259840
  1821.0 387.1 %reduce-scatter.7.cloned.1.call-start = ((), (), s32[]{:S(2)}) async-start(), calls=%async_computation.6 | async-start | bytes 1310720 | tf_op jit(solution)/shard_map/reduce_scatter | solution.py:162
  1825.0 410.2 %reduce-scatter.11.cloned.1.call-start = ((), (), s32[]{:S(2)}) async-start(), calls=%async_computation.9 | async-start | bytes 1310720 | tf_op jit(solution)/shard_map/reduce_scatter | solution.py:258
  1825.3 3.8 copy-start.1
Sparse Core Ops, SparseCore 0:
  9.9 25.8 all-gather.7
  39.7 100.3 all-gather.3
  144.2 98.8 all-gather.5
  1073.5 736.7 reduce-scatter.8
  1821.1 363.1 reduce-scatter.12
  2187.5 20.6 reduce-scatter.6
  2211.3 23.8 reduce-scatter.10
where the time goes:
time: 2280 us; the launch traced here: 2240 us
  waiting for transfers between devices  1250 us (55%)
  local copies, waits for them, and re-layouts  452 us (20%)
  other arithmetic  252 us (11%)
  loops' own time  238 us (10%)
  matrix products  34.8 us (2%)
    reduce_scatter x1, waiting for transfers between devices, shards(): lax.psum_scatter(key_terms.reshape(context_count * length, 2 * kv_width),...  737 us
    unnamed x8, waiting for transfers between devices  353 us
    dynamic_update_slice x64, local copies, waits for them, and re-layouts, shards(): lax.scan(back_block, jnp.zeros((local_kv, group_size, length, head_width)...  300 us
    another operation x2, loops' own time, over_blocks(): return lax.scan(step_block, running, block_items)[0]  156 us
    dynamic_slice x192, local copies, waits for them, and re-layouts, over_blocks(): return lax.scan(step_block, running, block_items)[0]  112 us
    all_gather x1, waiting for transfers between devices, shards(): lax.all_gather(keys_here, 'context', axis=0, tiled=True)  100 us
    add x64, other arithmetic, stats_block(): key_positions = first_row + jnp.arange(key_block.shape[0], dtype=jnp.int32)  83.8 us
    add x64, other arithmetic, back_block(): key_positions = offset + jnp.arange(length, dtype=jnp.int32)  81.7 us
  transfers between devices with their start and end apart: 7, of which 6 were waited for; matrix products, arithmetic and copies ran while one was open for 7% of the time, Pallas kernels for 0%

commit v1 on v0

v1 whole, which is shorter than its diff:
```python
import jax
import jax.numpy as jnp
from jax import lax
from jax.experimental import pallas as pl
from jax.experimental.pallas import tpu as pltpu
from jax.sharding import PartitionSpec as P

HD = 128
THETA = 500000.0
LOG2E = 1.4426950408889634
NEGATIVE = -1e30
NY, NX, NZ = 2, 4, 8
TILE = 512
F32, BF16 = jnp.float32, jnp.bfloat16


def position():
    rank = lax.axis_index("context")
    return rank // (NX * NZ), (rank // NZ) % NX, rank % NZ


def rank_of(y, x, z):
    return (y * NX + x) * NZ + z


def turn(value, step, count):
    return lax.rem(value + (step + count), count)


def remote(source, target, send_sem, recv_sem, rank):
    return pltpu.make_async_remote_copy(
        src_ref=source,
        dst_ref=target,
        send_sem=send_sem,
        recv_sem=recv_sem,
        device_id={"context": rank},
        device_id_type=pl.DeviceIdType.MESH,
    )


def greet(y, x, z):
    barrier = pltpu.get_barrier_semaphore()
    ranks = [rank_of(1 - y, x, z), rank_of(y, x, turn(z, 1, NZ)), rank_of(y, x, turn(z, -1, NZ))]
    ranks += [rank_of(y, turn(x, step, NX), z) for step in (1, 2, 3)]
    for rank in ranks:
        pl.semaphore_signal(
            barrier, inc=1, device_id={"context": rank}, device_id_type=pl.DeviceIdType.MESH
        )
    pl.semaphore_wait(barrier, len(ranks))


CHAINS = ((1, 0, "long"), (1, 1, "short"), (-1, 1, "long"), (-1, 0, "short"))


def gather_kernel(
    k_in, v_in, k_all, v_all, y_send, y_recv, kx_send, kx_recv, vz_send, vz_recv, kz_send, kz_recv,
    vx_send, vx_recv,
):
    y, x, z = position()
    k_all[y, x, z] = k_in[...]
    v_all[y, x, z] = v_in[...]
    greet(y, x, z)
    started = []

    def go(copy):
        copy.start()
        started.append(copy)
        return copy

    partner = rank_of(1 - y, x, z)
    k_pair = go(remote(k_in, k_all.at[y, x, z], y_send.at[0], y_recv.at[0], partner))
    v_pair = go(remote(v_in, v_all.at[y, x, z], y_send.at[1], y_recv.at[1], partner))

    def vz_hop(chain, hop):
        way, half, _ = CHAINS[chain]
        part = v_all.at[half, x, turn(z, -way * hop, NZ)]
        return go(
            remote(
                part, part, vz_send.at[chain, hop], vz_recv.at[chain, hop],
                rank_of(y, x, turn(z, way, NZ)),
            )
        )

    def kz_hop(chain, hop):
        way, half, _ = CHAINS[chain]
        part = k_all.at[half, :, turn(z, -way * hop, NZ)]
        return go(
            remote(
                part, part, kz_send.at[chain, hop], kz_recv.at[chain, hop],
                rank_of(y, x, turn(z, way, NZ)),
            )
        )

    def vx_hop(chain, hop):
        way, half, _ = CHAINS[chain]
        part = v_all.at[half, turn(x, -way * hop, NX)]
        return go(
            remote(
                part, part, vx_send.at[chain, hop], vx_recv.at[chain, hop],
                rank_of(y, turn(x, way, NX), z),
            )
        )

    k_pair.wait_recv()
    kx = []
    for step in (1, 2, 3):
        part = k_all.at[:, x, z]
        kx.append(
            go(
                remote(
                    part, part, kx_send.at[step - 1], kx_recv.at[step - 1],
                    rank_of(y, turn(x, step, NX), z),
                )
            )
        )
    v_pair.wait_recv()
    all_chains, long_chains = (0, 1, 2, 3), (0, 2)
    vz = {chain: vz_hop(chain, 0) for chain in all_chains}
    for copy in kx:
        copy.wait_recv()
    kz = {chain: kz_hop(chain, 0) for chain in all_chains}

    def advance(flight, hop_of, hop, chains):
        for chain in chains:
            flight[chain].wait_recv()
            flight[chain] = hop_of(chain, hop)

    advance(vz, vz_hop, 1, all_chains)
    advance(vz, vz_hop, 2, all_chains)
    advance(kz, kz_hop, 1, all_chains)
    advance(vz, vz_hop, 3, long_chains)
    for chain in all_chains:
        vz[chain].wait_recv()
    vx = {chain: vx_hop(chain, 0) for chain in all_chains}
    advance(kz, kz_hop, 2, all_chains)
    advance(kz, kz_hop, 3, long_chains)
    for chain in long_chains:
        vx[chain].wait_recv()
        vx[chain] = vx_hop(chain, 1)
    for chain in all_chains:
        kz[chain].wait_recv()
        vx[chain].wait_recv()
    for copy in started:
        copy.wait_send()


def gather_blocks(key_rows, value_rows):
    rows = key_rows.shape[0]
    whole = jax.ShapeDtypeStruct((NY, NX, NZ, rows, HD), BF16)
    vmem = pl.BlockSpec(memory_space=pltpu.VMEM)
    dma = pltpu.SemaphoreType.DMA
    return pl.pallas_call(
        gather_kernel,
        out_shape=(whole, whole),
        in_specs=[vmem] * 2,
        out_specs=(vmem, vmem),
        scratch_shapes=[
            dma((2,)), dma((2,)), dma((3,)), dma((3,)), dma((4, 4)), dma((4, 4)), dma((4, 4)),
            dma((4, 4)), dma((4, 2)), dma((4, 2)),
        ],
        compiler_params=pltpu.CompilerParams(
            collective_id=1, has_side_effects=True, vmem_limit_bytes=24 * 2**20
        ),
        name="gather_blocks",
    )(key_rows, value_rows)


def add_into(target, term):
    target[...] = (target[...].astype(F32) + term[...].astype(F32)).astype(BF16)


def scatter_kernel(
    a_in, b_in, a_out, b_out, az_buf, bx_buf, bz_buf, a_sum, b_sum, ax_buf, a_low, b_low, y_buf,
    az_send, az_recv, bx_send, bx_recv, bz_send, bz_recv, ax_send, ax_recv, y_send, y_recv,
):
    y, x, z = position()
    greet(y, x, z)
    started = []

    def go(copy):
        copy.start()
        started.append(copy)
        return copy

    def az_hop(chain, hop, hops):
        way, half, _ = CHAINS[chain]
        far = turn(z, way * (hops - hop), NZ)
        own = a_in.at[half, :, far]
        source = own
        if hop:
            source = az_buf.at[chain, hop - 1]
            add_into(source, own)
        return go(
            remote(
                source, az_buf.at[chain, hop], az_send.at[chain, hop], az_recv.at[chain, hop],
                rank_of(y, x, turn(z, way, NZ)),
            )
        )

    def bx_hop(chain, hop, hops):
        way, half, _ = CHAINS[chain]
        far = turn(x, way * (hops - hop), NX)
        own = b_in.at[half, far]
        source = own
        if hop:
            source = bx_buf.at[chain, hop - 1]
            add_into(source, own)
        return go(
            remote(
                source, bx_buf.at[chain, hop], bx_send.at[chain, hop], bx_recv.at[chain, hop],
                rank_of(y, turn(x, way, NX), z),
            )
        )

    def bz_hop(chain, hop, hops):
        way, half, _ = CHAINS[chain]
        far = turn(z, way * (hops - hop), NZ)
        own = b_sum.at[half, far]
        source = own
        if hop:
            source = bz_buf.at[chain, hop - 1]
            add_into(source, own)
        return go(
            remote(
                source, bz_buf.at[chain, hop], bz_send.at[chain, hop], bz_recv.at[chain, hop],
                rank_of(y, x, turn(z, way, NZ)),
            )
        )

    z_hops = {0: 4, 1: 3, 2: 4, 3: 3}
    x_hops = {0: 2, 1: 1, 2: 2, 3: 1}
    order = (0, 2, 1, 3)
    az = {chain: az_hop(chain, 0, z_hops[chain]) for chain in order}
    bx = {chain: bx_hop(chain, 0, x_hops[chain]) for chain in order}

    def advance(flight, hop_of, hop, hops):
        for chain in order:
            if hop < hops[chain]:
                flight[chain].wait_recv()
                flight[chain] = hop_of(chain, hop, hops[chain])

    advance(az, az_hop, 1, z_hops)
    advance(bx, bx_hop, 1, x_hops)
    advance(az, az_hop, 2, z_hops)
    for chain in order:
        bx[chain].wait_recv()
    for half in range(NY):
        right, left = (0, 3) if half == 0 else (1, 2)
        b_sum[half] = (
            b_in[half, x].astype(F32)
            + bx_buf[right, x_hops[right] - 1].astype(F32)
            + bx_buf[left, x_hops[left] - 1].astype(F32)
        ).astype(BF16)
    bz = {chain: bz_hop(chain, 0, z_hops[chain]) for chain in order}
    advance(az, az_hop, 3, z_hops)
    advance(bz, bz_hop, 1, z_hops)
    for chain in order:
        az[chain].wait_recv()
    for half in range(NY):
        right, left = (0, 3) if half == 0 else (1, 2)
        a_sum[:, half] = (
            a_in[half, :, z].astype(F32)
            + az_buf[right, z_hops[right] - 1].astype(F32)
            + az_buf[left, z_hops[left] - 1].astype(F32)
        ).astype(BF16)
    ax = []
    for step in (1, 2, 3):
        other = turn(x, step, NX)
        ax.append(
            go(
                remote(
                    a_sum.at[other], ax_buf.at[step - 1], ax_send.at[step - 1],
                    ax_recv.at[step - 1], rank_of(y, other, z),
                )
            )
        )
    advance(bz, bz_hop, 2, z_hops)
    for copy in ax:
        copy.wait_recv()
    a_total = a_sum[x].astype(F32)
    for step in range(3):
        a_total = a_total + ax_buf[step].astype(F32)
    a_low[...] = a_total.astype(BF16)
    partner = rank_of(1 - y, x, z)
    a_pair = go(remote(a_low.at[1 - y], y_buf.at[0], y_send.at[0], y_recv.at[0], partner))
    advance(bz, bz_hop, 3, z_hops)
    for chain in order:
        bz[chain].wait_recv()
    for half in range(NY):
        right, left = (0, 3) if half == 0 else (1, 2)
        b_low[half] = (
            b_sum[half, z].astype(F32)
            + bz_buf[right, z_hops[right] - 1].astype(F32)
            + bz_buf[left, z_hops[left] - 1].astype(F32)
        ).astype(BF16)
    b_pair = go(remote(b_low.at[1 - y], y_buf.at[1], y_send.at[1], y_recv.at[1], partner))
    a_pair.wait_recv()
    a_out[...] = a_low[y].astype(F32) + y_buf[0].astype(F32)
    b_pair.wait_recv()
    b_out[...] = b_low[y].astype(F32) + y_buf[1].astype(F32)
    for copy in started:
        copy.wait_send()


def scatter_blocks(a_parts, b_parts, identity, name):
    rows = a_parts.shape[-2]
    one = jax.ShapeDtypeStruct((rows, HD), F32)
    vmem = pl.BlockSpec(memory_space=pltpu.VMEM)
    dma = pltpu.SemaphoreType.DMA

    def room(*lead):
        return pltpu.VMEM(lead + (rows, HD), BF16)

    return pl.pallas_call(
        scatter_kernel,
        out_shape=(one, one),
        in_specs=[vmem] * 2,
        out_specs=(vmem, vmem),
        scratch_shapes=[
            room(4, 4, NX), room(4, 2, NZ), room(4, 4), room(NX, NY), room(NY, NZ), room(3, NY),
            room(NY), room(NY), room(2),
            dma((4, 4)), dma((4, 4)), dma((4, 2)), dma((4, 2)), dma((4, 4)), dma((4, 4)),
            dma((3,)), dma((3,)), dma((2,)), dma((2,)),
        ],
        compiler_params=pltpu.CompilerParams(
            collective_id=identity, has_side_effects=True, vmem_limit_bytes=32 * 2**20
        ),
        name=name,
    )(a_parts, b_parts)


def matmul(left, right, left_dim, right_dim):
    return lax.dot_general(
        left, right, (((left_dim,), (right_dim,)), ((), ())), preferred_element_type=F32
    )


def attention_kernel(q_ref, k_ref, v_ref, do_ref, o_ref, dq_ref, dk_ref, dv_ref, weights):
    length = q_ref.shape[0]
    heads = q_ref.shape[1] // HD
    columns = heads * length
    rank = lax.axis_index("context")
    first = rank * length
    full = first // TILE
    scale = HD ** (-0.5)
    factor = scale * LOG2E

    def stack(ref):
        return jnp.concatenate([ref[:, h * HD : (h + 1) * HD] for h in range(heads)], axis=0)

    queries = stack(q_ref)
    last_rows = pl.ds(pl.multiple_of(full * TILE, TILE), TILE)

    def rows_of(index):
        return pl.ds(pl.multiple_of(index * TILE, TILE), TILE)

    key_at = full * TILE + lax.broadcasted_iota(jnp.int32, (TILE, columns), 0)
    query_at = first + lax.rem(lax.broadcasted_iota(jnp.int32, (TILE, columns), 1), length)
    visible = key_at <= query_at

    def scores(rows):
        return matmul(k_ref[rows, :], queries, 1, 1)

    def max_step(index, current):
        return jnp.maximum(current, jnp.max(scores(rows_of(index)), axis=0, keepdims=True))

    top = jnp.max(jnp.where(visible, scores(last_rows), NEGATIVE), axis=0, keepdims=True)
    top = lax.fori_loop(0, full, max_step, top)
    top = top * factor

    def weigh(rows, current, masked):
        totals, output = current
        exponent = scores(rows) * factor - top
        if masked:
            exponent = jnp.where(visible, exponent, NEGATIVE)
        weight = jnp.exp2(exponent)
        totals = totals + jnp.sum(weight, axis=0, keepdims=True)
        low = weight.astype(BF16)
        weights[rows, :] = low
        return totals, output + matmul(v_ref[rows, :], low, 0, 0)

    start = (jnp.zeros((1, columns), F32), jnp.zeros((HD, columns), F32))
    start = weigh(last_rows, start, True)
    totals, output = lax.fori_loop(
        0, full, lambda index, current: weigh(rows_of(index), current, False), start
    )
    inverse = 1.0 / totals
    output = (output * inverse).astype(BF16).astype(F32)
    cotangent = stack(do_ref).astype(F32).T
    delta = jnp.sum(cotangent * output, axis=0, keepdims=True) * inverse
    scaled = cotangent * inverse
    scaled_across = scaled.astype(BF16)
    scaled_rows = scaled.T.astype(BF16)
    output_rows = output.T.astype(BF16)
    for h in range(heads):
        o_ref[:, h * HD : (h + 1) * HD] = output_rows[h * length : (h + 1) * length]

    def back(index, query_grad):
        rows = rows_of(index)
        low = weights[rows, :]
        change = matmul(v_ref[rows, :], scaled_across, 1, 0) - delta
        score_grad = (low.astype(F32) * change).astype(BF16)
        dk_ref[rows, :] = (matmul(score_grad, queries, 1, 0) * scale).astype(BF16)
        dv_ref[rows, :] = matmul(low, scaled_rows, 1, 0).astype(BF16)
        return query_grad + matmul(k_ref[rows, :], score_grad, 0, 0)

    query_grad = lax.fori_loop(0, full + 1, back, jnp.zeros((HD, columns), F32))
    grad_rows = query_grad.T * scale
    for h in range(heads):
        dq_ref[:, h * HD : (h + 1) * HD] = grad_rows[h * length : (h + 1) * length]

    @pl.loop(full + 1, k_ref.shape[0] // TILE)
    def _(index):
        rows = rows_of(index)
        dk_ref[rows, :] = jnp.zeros((TILE, HD), BF16)
        dv_ref[rows, :] = jnp.zeros((TILE, HD), BF16)


def attention(queries, keys, values, cotangent):
    length, width = queries.shape
    tokens = keys.shape[0]
    vmem = pl.BlockSpec(memory_space=pltpu.VMEM)
    columns = width // HD * length
    return pl.pallas_call(
        attention_kernel,
        out_shape=(
            jax.ShapeDtypeStruct((length, width), BF16),
            jax.ShapeDtypeStruct((length, width), F32),
            jax.ShapeDtypeStruct((tokens, HD), BF16),
            jax.ShapeDtypeStruct((tokens, HD), BF16),
        ),
        in_specs=[vmem] * 4,
        out_specs=(vmem,) * 4,
        scratch_shapes=[pltpu.VMEM((tokens, columns), BF16)],
        compiler_params=pltpu.CompilerParams(vmem_limit_bytes=48 * 2**20),
        cost_estimate=pl.CostEstimate(
            flops=14 * tokens * columns * HD, bytes_accessed=9 * 2**20, transcendentals=tokens * columns
        ),
        name="attention",
    )(queries, keys, values, cotangent)


def rope_tables(positions, head_width):
    half_width = head_width // 2
    exponent = jnp.arange(half_width, dtype=F32) * (2.0 / head_width)
    frequency = jnp.power(jnp.float32(THETA), -exponent)
    angles = positions.astype(F32)[:, None] * frequency[None, :]
    return (jnp.cos(angles), jnp.sin(angles))


def rotate(field, cosine_table, sine_table):
    half_width = field.shape[-1] // 2
    first_half = field[..., :half_width]
    second_half = field[..., half_width:]
    cosine_part = cosine_table[:, None, :]
    sine_part = sine_table[:, None, :]
    return jnp.concatenate(
        [
            first_half * cosine_part - second_half * sine_part,
            second_half * cosine_part + first_half * sine_part,
        ],
        axis=-1,
    )


def shards(hidden_in, value_first, w_query, w_key, w_value, w_out, value_mix, grad_out):
    tensor_count = lax.axis_size("tensor")
    context_rank = lax.axis_index("context")
    length, model_width = hidden_in.shape[1:]
    heads = w_query.shape[1] // HD
    share_rows = length // tensor_count
    inputs = hidden_in.reshape(length, model_width)
    firsts = value_first.reshape(length, HD)
    block_rows = context_rank * length + jnp.arange(length, dtype=jnp.int32)
    cosines, sines = rope_tables(block_rows, HD)

    def turned(field, sine_table):
        count = field.shape[1] // HD
        return (
            rotate(field.reshape(length, count, HD), cosines, sine_table)
            .astype(BF16)
            .reshape(length, count * HD)
        )

    keys = turned(jnp.dot(inputs, w_key, preferred_element_type=F32), sines)
    projected = jnp.dot(inputs, w_value, preferred_element_type=F32)
    mixed = (value_mix[0] * projected + value_mix[1] * firsts.astype(F32)).astype(BF16)
    keys_all, values_all = gather_blocks(keys, mixed)
    queries = turned(jnp.dot(inputs, w_query, preferred_element_type=F32), sines)
    grads = lax.all_gather(grad_out, "tensor", axis=1, tiled=True).reshape(length, model_width)
    cotangent = matmul(grads, w_out, 1, 1).astype(BF16)
    outputs, query_grad, key_parts, value_parts = attention(
        queries, keys_all.reshape(-1, HD), values_all.reshape(-1, HD), cotangent
    )
    attn_out = lax.psum_scatter(
        jnp.dot(outputs, w_out, preferred_element_type=F32).astype(BF16),
        "tensor",
        scatter_dimension=0,
        tiled=True,
    ).reshape(1, share_rows, model_width)
    blocks = (NY, NX, NZ, length, HD)
    key_sum, value_sum = scatter_blocks(
        key_parts.reshape(blocks), value_parts.reshape(blocks), 2, "scatter_grads"
    )
    query_pre = turned(query_grad, -sines)
    key_pre = turned(key_sum, -sines)
    value_pre = (value_mix[0] * value_sum).astype(BF16)
    first_grad = (value_mix[1] * value_sum).astype(BF16).reshape(1, length, HD)
    summed = matmul(query_pre, w_query, 1, 1)
    summed = summed + matmul(key_pre, w_key, 1, 1)
    grad_in = lax.psum_scatter(
        (summed + matmul(value_pre, w_value, 1, 1)).astype(BF16),
        "tensor",
        scatter_dimension=0,
        tiled=True,
    ).reshape(1, share_rows, model_width)
    strips = (NY, NX, NZ, model_width // (NY * NX * NZ), HD)
    key_weight, value_weight = scatter_blocks(
        matmul(inputs, key_pre, 0, 0).astype(BF16).reshape(strips),
        matmul(inputs, value_pre, 0, 0).astype(BF16).reshape(strips),
        3,
        "scatter_weights",
    )
    return (attn_out, grad_in, first_grad, key_weight, value_weight)


def solution(mesh):
    return jax.shard_map(
        shards,
        mesh=mesh,
        in_specs=(
            P("context", None, None),
            P("context", None, "tensor"),
            P(None, "tensor"),
            P(None, "tensor"),
            P(None, "tensor"),
            P("tensor", None),
            P(None, "tensor"),
            P("context", "tensor", None),
        ),
        out_specs=(
            P("context", "tensor", None),
            P("context", "tensor", None),
            P("context", None, "tensor"),
            P("context", "tensor"),
            P("context", "tensor"),
        ),
        check_vma=False,
    )
```

time: 2280 us -> 195 us (0.09); the launches traced: 2240 us -> 195 us
  waiting for transfers between devices: 1250 us -> 0.72 us
  local copies, waits for them, and re-layouts: 452 us -> 17 us
  other arithmetic: 252 us -> 3.87 us
  loops' own time: 238 us -> 0 us
  Pallas kernels: 0 us -> 140 us
    reduce_scatter x3 -> x2, waiting for transfers between devices: 786 us -> 0.01 us  [the longest x1 0.01 us: shards(): lax.psum_scatter(jnp.dot(outputs, w_out, preferred_element_type=F32).asty...]
    unnamed x8 -> x3, waiting for transfers between devices: 353 us -> 0.71 us
    dynamic_update_slice x64 -> x0, local copies, waits for them, and re-layouts: 300 us -> none  [shards(): lax.scan(back_block, jnp.zeros((local_kv, group_size, length, head_width)...]
    add x195 -> x0, other arithmetic: 247 us -> none  [the longest x64 83.8 us: stats_block(): key_positions = first_row + jnp.arange(key_block.shape[0], dtype=jnp.int32)]
    another operation x195 -> x0, loops' own time: 238 us -> none  [the longest x2 156 us: over_blocks(): return lax.scan(step_block, running, block_items)[0]]
    pallas_call x0 -> x4, Pallas kernels: none -> 140 us  [the longest x2 87.7 us: scatter_blocks(): pl.pallas_call(scatter_kernel, out_shape=(one, one), in_specs=[vmem] * 2,...]
    dynamic_slice x192 -> x0, local copies, waits for them, and re-layouts: 112 us -> none  [over_blocks(): return lax.scan(step_block, running, block_items)[0]]
    all_gather x2 -> x0, waiting for transfers between devices: 100 us -> none  [the longest x1 100 us: shards(): lax.all_gather(keys_here, 'context', axis=0, tiled=True)]
  transfers between devices with their start and end apart: 7 -> 3, of which waited for: 6 -> 0; matrix products, arithmetic and copies ran while one was open for 7% -> 14% of each run, Pallas kernels for 0% -> 69%
where the time goes in v1:
time: 195 us
  Pallas kernels  140 us (72%)
  matrix products  18.8 us (10%)
  local copies, waits for them, and re-layouts  17 us (9%)
  between operations  14.1 us (7%)
  other arithmetic  3.87 us (2%)
    pallas_call x2, Pallas kernels, scatter_blocks(): pl.pallas_call(scatter_kernel, out_shape=(one, one), in_specs=[vmem] * 2,...  87.7 us
    pallas_call x1, Pallas kernels, gather_blocks(): pl.pallas_call(gather_kernel, out_shape=(whole, whole), in_specs=[vmem] *...  47.5 us
    dot_general x6, matrix products, matmul(): lax.dot_general(left, right, (((left_dim,), (right_dim,)), ((), ())), pre...  11.5 us
    unnamed x34, local copies, waits for them, and re-layouts  6.83 us
    dot_general x1, local copies, waits for them, and re-layouts, shards(): jnp.dot(inputs, w_query, preferred_element_type=F32)  6.39 us
    pallas_call x1, Pallas kernels, attention(): pl.pallas_call(attention_kernel, out_shape=(jax.ShapeDtypeStruct((length,...  4.66 us
  transfers between devices with their start and end apart: 3, of which 0 were waited for; matrix products, arithmetic and copies ran while one was open for 14% of the time, Pallas kernels for 69%

profile of v1, /device:TPU:32, one launch (start us, length us, event | category | flops | bytes accessed | tf_op | source)
XLA Modules:
  0.0 194.7 jit_solution(12346693758660103031)
XLA Ops:
  7.2 0.0 copy-start
  7.2 0.0 all-gather.2.cloned.1.call-start
  7.2 0.7 all-gather.2.cloned.1.call-update
  7.9 0.0 reduce-scatter.3.cloned.1.call-start
  8.0 6.4 %copy.21 = bf16[512,4096]{1,0:T(8,128)(2,1)} copy(bf16[512,4096]{0,1:T(8,128)(2,1)} %bitcast.66) | data formatting | bytes 8388608 | tf_op jit(solution)/shard_map/dot_general | solution.py:489
  14.4 0.0 copy-done
  14.4 3.5 %fusion.6 = f32[128,4,128]{0,2,1:T(8,128)S(1)} fusion(bf16[4,128,4096]{2,1,0:T(8,128)(2,1)} %bitcast.67, bf16[1,128,4096]{2,1,0:T(8,128)(2,1)S(1)} %copy-done), kind=kOutput, calls=%fused_computation.14 | convolution fusion | flops 536870912 | bytes 5505024 | tf_op jit(solution)/shard_map/dot_general | solution.py:489
  17.9 0.0 copy-start.7
  17.9 0.0 copy-start.14
  18.0 0.8 fusion.34
  18.8 0.5 copy-done.11
  19.4 0.1 copy.22.q_ref
  19.5 0.6 fusion.37
  20.1 0.4 convolution_bitcast_fusion
  20.5 0.3 fusion.31
  20.9 0.1 pad_maximum_fusion.2.k_in
  21.0 1.7 fusion.4.v_in
  22.7 47.5 %gather_blocks.1 = (bf16[2,4,8,128,128]{4,3,2,1,0:T(8,128)(2,1)S(1)}, bf16[2,4,8,128,128]{4,3,2,1,0:T(8,128)(2,1)S(1)}) custom-call(bf16[128,128]{1,0:T(8,128)(2,1)S(1)} %pad_maximum_fusion.2.k_in, bf16[128,128]{1,0:T(8,128)(2,1)S(1)} %fusion.4.v_in), custom_call_target="tpu_custom_call" | custom-call | tf_op jit(solution)/shard_map/gather_blocks/pallas_call | solution.py:152
  70.2 1.3 copy-done.3
  71.5 4.8 %convolution_convert_fusion.3.do_ref = bf16[128,512]{1,0:T(8,128)(2,1)S(1)} fusion(bf16[512,4096]{1,0:T(8,128)(2,1)} %param.13, bf16[1,128,4096]{2,1,0:T(8,128)(2,1)} %all-gather.2.cloned.1.call-done), kind=kOutput, calls=%fused_computation.8 | convolution fusion | flops 536936448 | bytes 5373952 | tf_op jit(solution)/shard_map/dot_general | solution.py:333
  76.3 0.0 copy-start.5
  76.4 4.7 %attention.1 = (bf16[128,512]{1,0:T(8,128)(2,1)S(1)}, f32[128,512]{1,0:T(8,128)S(1)}, bf16[8192,128]{1,0:T(8,128)(2,1)S(1)}, bf16[8192,128]{1,0:T(8,128)(2,1)S(1)}) custom-call(bf16[128,512]{1,0:T(8,128)(2,1)S(1)} %copy.22.q_ref, bf16[8192,128]{1,0:T(8,128)(2,1)} %bitcast.64, bf16[8192,128]{1,0:T(8,128)(2,1)} %bitcast.65, ...), custom_call_target="tpu_custom_call" | custom-call | flops 7516192768 | bytes 9437184 | tf_op jit(solution)/shard_map/attention/pallas_call | solution.py:424
  81.0 1.3 copy-done.1
  82.4 1.7 convolution_convert_fusion.2
  84.1 0.0 reduce-scatter.3.cloned.1.call-update
  84.1 0.2 reduce-scatter.5.cloned.1.call-start
  84.3 0.0 copy-start.12
  84.3 0.0 copy-start.13
  84.4 0.8 copy.23
  85.2 1.6 copy-done.2
  86.8 58.3 %scatter_grads.1 = (f32[128,128]{1,0:T(8,128)S(1)}, f32[128,128]{1,0:T(8,128)S(1)}) custom-call(bf16[2,4,8,128,128]{4,3,2,1,0:T(8,128)(2,1)S(1)} %bitcast.61, bf16[2,4,8,128,128]{4,3,2,1,0:T(8,128)(2,1)S(1)} %bitcast.62), custom_call_target="tpu_custom_call" | custom-call | tf_op jit(solution)/shard_map/scatter_grads/pallas_call | solution.py:314
  145.1 1.0 subtract_convert_fusion
  146.1 0.3 fusion.33
  146.4 0.0 copy-start.10
  146.5 1.5 fusion.38
  148.0 0.0 copy-start.8
  148.0 0.5 convolution_add_fusion.1
  148.5 0.7 copy-done.8
  149.2 2.1 %fusion = bf16[128,4096]{1,0:T(8,128)(2,1)} fusion(f32[128,4096]{1,0:T(8,128)S(1)} %convolution_add_fusion.1, bf16[4096,128]{1,0:T(8,128)(2,1)S(1)} %copy-done.8, f32[128,128]{1,0:T(8,128)S(1)} %get-tuple-element.22, f32[]{:T(128)} %bitcast.8), kind=kOutput, calls=%fused_computation.2 | convolution fusion | flops 135299072 | bytes 4259844 | tf_op jit(solution)/shard_map/dot_general | solution.py:333
  151.3 0.0 reduce-scatter.5.cloned.1.call-update
  151.3 0.5 fusion.1
  151.9 0.7 copy.18
  152.5 2.1 %fusion.2 = bf16[4096,128]{0,1:T(8,128)(2,1)} fusion(bf16[1,128,4096]{2,1,0:T(8,128)(2,1)S(1)} %copy-done, f32[128,128]{1,0:T(8,128)S(1)} %get-tuple-element.22, f32[]{:T(128)} %bitcast.8), kind=kOutput, calls=%fused_computation.7 | convolution fusion | flops 134774784 | bytes 2162692 | tf_op jit(solution)/shard_map/dot_general | solution.py:333
  154.6 1.6 copy.19
  156.2 29.4 %scatter_weights.1 = (f32[64,128]{1,0:T(8,128)S(1)}, f32[64,128]{1,0:T(8,128)S(1)}) custom-call(bf16[2,4,8,64,128]{4,3,2,1,0:T(8,128)(2,1)S(1)} %bitcast.59, bf16[2,4,8,64,128]{4,3,2,1,0:T(8,128)(2,1)S(1)} %bitcast.60), custom_call_target="tpu_custom_call" | custom-call | tf_op jit(solution)/shard_map/scatter_weights/pallas_call | solution.py:314
  185.7 1.2 fusion.29
  186.9 0.6 copy.26
  187.5 0.6 copy.27
  (26 shorter events, 0.1 us)
Async XLA Ops:
  7.2 7.2 %copy-start = (bf16[1,128,4096]{2,1,0:T(8,128)(2,1)S(1)}, bf16[1,128,4096]{2,1,0:T(8,128)(2,1)}, u32[]{:S(2)}) copy-start(bf16[1,128,4096]{2,1,0:T(8,128)(2,1)} %param.8) | copy-start | bytes 3145732
  7.2 64.4 %all-gather.2.cloned.1.call-start = ((), (), s32[]{:S(2)}) async-start(), calls=%async_computation.2 | async-start | bytes 1310720 | tf_op jit(solution)/shard_map/all_gather | solution.py:490
  7.9 179.0 %reduce-scatter.3.cloned.1.call-start = ((), (), s32[]{:S(2)}) async-start(), calls=%async_computation.3 | async-start | bytes 1310720 | tf_op jit(solution)/shard_map/reduce_scatter | solution.py:495
  14.4 5.1 %copy-start.15 = (f32[2,1]{0,1:T(1,128)S(1)}, f32[2,1]{0,1:T(1,128)}, u32[]{:S(2)}) copy-start(f32[2,1]{0,1:T(1,128)} %param.14) | copy-start | bytes 28
  14.4 5.7 %copy-start.9 = (bf16[4096,128]{1,0:T(8,128)(2,1)S(1)}, bf16[4096,128]{1,0:T(8,128)(2,1)}, u32[]{:S(2)}) copy-start(bf16[4096,128]{1,0:T(8,128)(2,1)} %param.11) | copy-start | bytes 3145732
  17.9 3.0 %copy-start.7 = (bf16[4096,128]{1,0:T(8,128)(2,1)S(1)}, bf16[4096,128]{1,0:T(8,128)(2,1)}, u32[]{:S(2)}) copy-start(bf16[4096,128]{1,0:T(8,128)(2,1)} %param.12) | copy-start | bytes 3145732
  17.9 3.0 %copy-start.14 = (bf16[1,128,128]{2,1,0:T(8,128)(2,1)S(1)}, bf16[1,128,128]{2,1,0:T(8,128)(2,1)}, u32[]{:S(2)}) copy-start(bf16[1,128,128]{2,1,0:T(8,128)(2,1)} %param.9) | copy-start | bytes 98308
  18.8 0.6 copy-start.11
  70.2 1.3 copy-start.3
  71.5 4.8 %copy-start.4 = (bf16[2,4,8,128,128]{4,3,2,1,0:T(8,128)(2,1)}, bf16[2,4,8,128,128]{4,3,2,1,0:T(8,128)(2,1)S(1)}, u32[]{:S(2)}) copy-start(bf16[2,4,8,128,128]{4,3,2,1,0:T(8,128)(2,1)S(1)} %get-tuple-element.16) | copy-start | bytes 6291460
  76.3 6.0 %copy-start.5 = (bf16[512,4096]{1,0:T(8,128)(2,1)S(1)}, bf16[512,4096]{1,0:T(8,128)(2,1)}, u32[]{:S(2)}) copy-start(bf16[512,4096]{1,0:T(8,128)(2,1)} %param.13) | copy-start | bytes 12582916
  81.0 1.3 copy-start.1
  84.1 102.8 %reduce-scatter.5.cloned.1.call-start = ((), (), s32[]{:S(2)}) async-start(), calls=%async_computation.4 | async-start | bytes 1310720 | tf_op jit(solution)/shard_map/reduce_scatter | solution.py:511
  84.3 60.7 %copy-start.12 = (f32[128,64]{0,1:T(8,128)S(1)}, f32[128,64]{0,1:T(8,128)}, u32[]{:S(2)}) copy-start(f32[128,64]{0,1:T(8,128)} %copy-done.11) | copy-start | bytes 98308
  84.3 60.7 %copy-start.13 = (f32[128,64]{0,1:T(8,128)S(1)}, f32[128,64]{0,1:T(8,128)}, u32[]{:S(2)}) copy-start(f32[128,64]{0,1:T(8,128)} %get-tuple-element.33) | copy-start | bytes 98308
  85.2 1.6 copy-start.2
  86.8 59.7 %copy-start.6 = (bf16[4096,512]{1,0:T(8,128)(2,1)S(1)}, bf16[4096,512]{1,0:T(8,128)(2,1)}, u32[]{:S(2)}) copy-start(bf16[4096,512]{1,0:T(8,128)(2,1)} %param.10) | copy-start | bytes 12582916
  146.4 1.6 copy-start.10
  148.0 1.2 copy-start.8
Sparse Core Ops, SparseCore 0:
  9.8 27.0 all-gather.1
  84.2 42.3 reduce-scatter.2
  151.5 20.2 reduce-scatter.4

commit v2 on v0

v2 whole, which is shorter than its diff:
```python
import jax
import jax.numpy as jnp
from jax import lax
from jax.experimental import pallas as pl
from jax.experimental.pallas import tpu as pltpu
from jax.sharding import PartitionSpec as P

HD = 128
THETA = 500000.0
LOG2E = 1.4426950408889634
NEGATIVE = -1e30
NY, NX, NZ = 2, 4, 8
NH = NZ // 2
F32, BF16 = jnp.float32, jnp.bfloat16

CHAINS = ((1, 0, 4, 2), (1, 1, 3, 1), (-1, 1, 4, 2), (-1, 0, 3, 1))
ORDER = (0, 2, 1, 3)
ARRIVE = ((0, 3), (1, 2))


def rank_of(y, x, z):
    return (y * NX + x) * NZ + z


def turn(value, step, count):
    return lax.rem(value + (step + count), count)


def when(condition, action):
    if condition is True:
        action()
    else:
        pl.when(condition)(action)


def matmul(left, right, left_dim, right_dim):
    return lax.dot_general(
        left, right, (((left_dim,), (right_dim,)), ((), ())), preferred_element_type=F32
    )


def add_into(target, term):
    target[...] = (target[...].astype(F32) + term[...].astype(F32)).astype(BF16)


class Sender:
    def __init__(self):
        self.started = []

    def build(self, source, target, send_sem, recv_sem, axis, rank):
        return pltpu.make_async_remote_copy(
            src_ref=source,
            dst_ref=target,
            send_sem=send_sem,
            recv_sem=recv_sem,
            device_id={axis: rank},
            device_id_type=pl.DeviceIdType.MESH,
        )

    def go(self, copy, condition=True):
        copy.start()
        self.started.append((condition, copy))
        return copy

    def finish(self):
        for condition, copy in self.started:
            when(condition, copy.wait_send)


def gather_steps(send, place, k_own, v_own, k_all, v_all, sems):
    y, x, z, holder = place
    y_send, y_recv, kx_send, kx_recv, vz_send, vz_recv, kz_send, kz_recv, vx_send, vx_recv = sems
    slot = z // 2
    partner = rank_of(1 - y, x, z)
    lends = jnp.logical_not(holder(z))
    pairs = [
        send.build(own, whole.at[y, x, slot], y_send.at[i], y_recv.at[i], "context", partner)
        for i, (own, whole) in enumerate(((k_own, k_all), (v_own, v_all)))
    ]

    def lend():
        for copy in pairs:
            copy.start()

    def keep():
        k_all[y, x, slot] = k_own[...]
        v_all[y, x, slot] = v_own[...]

    pl.when(lends)(lend)
    pl.when(holder(z))(keep)
    send.started += [(lends, copy) for copy in pairs]

    kx = []
    for step in (1, 2, 3):
        part = k_all.at[:, x, slot]
        kx.append(
            send.build(
                part, part, kx_send.at[step - 1], kx_recv.at[step - 1], "context",
                rank_of(y, turn(x, step, NX), z),
            )
        )

    def z_hop(chain, hop, whole, lead, send_sem, recv_sem):
        way, half, _, _ = CHAINS[chain]
        origin = turn(z, -way * hop, NZ)
        part = whole.at[half, lead, origin // 2]
        copy = send.build(
            part, part, send_sem.at[chain, hop], recv_sem.at[chain, hop], "context",
            rank_of(y, x, turn(z, way, NZ)),
        )
        return holder(origin), copy

    def vz_hop(chain, hop):
        return z_hop(chain, hop, v_all, x, vz_send, vz_recv)

    def kz_hop(chain, hop):
        return z_hop(chain, hop, k_all, slice(None), kz_send, kz_recv)

    def vx_hop(chain, hop):
        way, half, _, _ = CHAINS[chain]
        part = v_all.at[half, turn(x, -way * hop, NX)]
        return True, send.build(
            part, part, vx_send.at[chain, hop], vx_recv.at[chain, hop], "context",
            rank_of(y, turn(x, way, NX), z),
        )

    def advance(hop_of, hop, ring):
        for chain in ORDER:
            if hop < CHAINS[chain][ring]:
                condition, copy = hop_of(chain, hop)

                def act():
                    if hop:
                        hop_of(chain, hop - 1)[1].wait_recv()
                    copy.start()

                when(condition, act)
                send.started.append((condition, copy))

    def drain(hop_of, ring, parity):
        for chain in ORDER:
            hops = CHAINS[chain][ring]
            condition = True
            if parity:
                condition = holder(turn(z, -CHAINS[chain][0] * hops, NZ))
            when(condition, hop_of(chain, hops - 1)[1].wait_recv)

    yield

    def pair_keys():
        pairs[0].wait_recv()
        for copy in kx:
            copy.start()
        pairs[1].wait_recv()

    pl.when(holder(z))(pair_keys)
    send.started += [(holder(z), copy) for copy in kx]
    advance(vz_hop, 0, 2)

    def row_keys():
        for copy in kx:
            copy.wait_recv()

    pl.when(holder(z))(row_keys)
    advance(kz_hop, 0, 2)
    advance(vz_hop, 1, 2)
    advance(vz_hop, 2, 2)
    advance(kz_hop, 1, 2)
    yield
    advance(vz_hop, 3, 2)
    drain(vz_hop, 2, True)
    advance(vx_hop, 0, 3)
    advance(kz_hop, 2, 2)
    yield
    advance(kz_hop, 3, 2)
    advance(vx_hop, 1, 3)
    yield
    drain(kz_hop, 2, True)
    drain(vx_hop, 3, False)
    yield


def scatter_steps(send, place, parity, a_in, b_in, a_out, b_out, bufs, sems):
    y, x, z, holder_of = place
    az_buf, bx_buf, bz_buf, a_sum, b_sum, ax_buf, low, y_buf = bufs
    az_send, az_recv, bx_send, bx_recv, bz_send, bz_recv, ax_send, ax_recv, y_send, y_recv = sems

    def holder(at):
        return holder_of(at) if parity else True

    def index(at):
        return at // 2 if parity else at

    def z_hop(chain, hop, own_of, buf, send_sem, recv_sem):
        way, half, hops, _ = CHAINS[chain]
        far = turn(z, way * (hops - hop), NZ)
        own = own_of(half, index(far))
        source = buf.at[chain, hop - 1] if hop else own
        copy = send.build(
            source, buf.at[chain, hop], send_sem.at[chain, hop], recv_sem.at[chain, hop],
            "context", rank_of(y, x, turn(z, way, NZ)),
        )
        return holder(far), own, copy

    def az_hop(chain, hop):
        return z_hop(chain, hop, lambda half, at: a_in.at[half, :, at], az_buf, az_send, az_recv)

    def bz_hop(chain, hop):
        return z_hop(chain, hop, lambda half, at: b_sum.at[half, at], bz_buf, bz_send, bz_recv)

    def bx_hop(chain, hop):
        way, half, _, hops = CHAINS[chain]
        own = b_in.at[half, turn(x, way * (hops - hop), NX)]
        source = bx_buf.at[chain, hop - 1] if hop else own
        copy = send.build(
            source, bx_buf.at[chain, hop], bx_send.at[chain, hop], bx_recv.at[chain, hop],
            "context", rank_of(y, turn(x, way, NX), z),
        )
        return True, own, copy

    def advance(hop_of, buf, hop, ring):
        for chain in ORDER:
            if hop < CHAINS[chain][ring]:
                condition, own, copy = hop_of(chain, hop)

                def act():
                    if hop:
                        hop_of(chain, hop - 1)[2].wait_recv()
                        add_into(buf.at[chain, hop - 1], own)
                    copy.start()

                when(condition, act)
                send.started.append((condition, copy))

    def drain(hop_of, ring):
        for chain in ORDER:
            hop_of(chain, CHAINS[chain][ring] - 1)[2].wait_recv()

    def total(own, buf, half, ring):
        right, left = ARRIVE[half]
        return (
            own.astype(F32)
            + buf[right, CHAINS[right][ring] - 1].astype(F32)
            + buf[left, CHAINS[left][ring] - 1].astype(F32)
        )

    partner = rank_of(1 - y, x, z)
    pairs = [
        send.build(
            low.at[i, 1 - y], y_buf.at[i], y_send.at[i], y_recv.at[i], "context", partner
        )
        for i in range(2)
    ]

    def hand_over(i, out):
        if parity:
            pl.when(holder(z))(pairs[i].start)
            send.started.append((holder(z), pairs[i]))
        else:
            send.go(pairs[i])

    def close(i, out):
        if parity:

            def keep():
                out[...] = low[i, y].astype(F32)

            def take():
                pairs[i].wait_recv()
                out[...] = y_buf[i].astype(F32)

            pl.when(holder(z))(keep)
            pl.when(jnp.logical_not(holder(z)))(take)
        else:
            pairs[i].wait_recv()
            out[...] = low[i, y].astype(F32) + y_buf[i].astype(F32)

    advance(az_hop, az_buf, 0, 2)
    advance(bx_hop, bx_buf, 0, 3)
    yield
    advance(az_hop, az_buf, 1, 2)
    advance(bx_hop, bx_buf, 1, 3)
    yield
    advance(az_hop, az_buf, 2, 2)
    drain(bx_hop, 3)
    for half in range(NY):
        b_sum[half] = total(b_in[half, x], bx_buf, half, 3).astype(BF16)
    advance(bz_hop, bz_buf, 0, 2)
    advance(az_hop, az_buf, 3, 2)
    advance(bz_hop, bz_buf, 1, 2)
    ax = []
    for step in (1, 2, 3):
        other = turn(x, step, NX)
        ax.append(
            send.build(
                a_sum.at[other], ax_buf.at[step - 1], ax_send.at[step - 1], ax_recv.at[step - 1],
                "context", rank_of(y, other, z),
            )
        )

    def a_ring():
        drain(az_hop, 2)
        for half in range(NY):
            a_sum[:, half] = total(a_in[half, :, index(z)], az_buf, half, 2).astype(BF16)
        for copy in ax:
            copy.start()

    when(holder(z), a_ring)
    send.started += [(holder(z), copy) for copy in ax]
    yield
    advance(bz_hop, bz_buf, 2, 2)

    def a_row():
        for copy in ax:
            copy.wait_recv()
        summed = a_sum[x].astype(F32)
        for step in range(3):
            summed = summed + ax_buf[step].astype(F32)
        low[0] = summed.astype(BF16)

    when(holder(z), a_row)
    hand_over(0, a_out)
    advance(bz_hop, bz_buf, 3, 2)
    yield

    def b_ring():
        drain(bz_hop, 2)
        for half in range(NY):
            low[1, half] = total(b_sum[half, index(z)], bz_buf, half, 2).astype(BF16)

    when(holder(z), b_ring)
    hand_over(1, b_out)
    close(0, a_out)
    close(1, b_out)
    yield


def block_kernel(
    x_hbm, first_ref, wq_hbm, wk_hbm, wv_hbm, wo_hbm, mix_ref, g_hbm, cos_ref, sin_ref,
    attn_ref, gin_ref, gfirst_ref, gwk_ref, gwv_ref,
    x_buf, wq, wk, wv, wo, g_all, xt, k_own, v_own, k_all, v_all, q_all, cot_all, weights,
    o_acc, dq_acc, o_send, o_recv, dq_send, dq_recv, stat_mine, stat_pair, dk_all, dv_all,
    k_sum, v_sum, part_out, recv_out, part_in, recv_in, acc_in, wk_part, wv_part,
    grad_bufs, weight_bufs, local_sem, gather_sems, grad_sems, weight_sems,
    pair_send, pair_recv, g_send, g_recv, out_send, out_recv, in_send, in_recv,
):
    rank = lax.axis_index("context")
    y, x, z = rank // (NX * NZ), (rank // NZ) % NX, rank % NZ
    tensor, tensors = lax.axis_index("tensor"), lax.axis_size("tensor")
    length, width = x_buf.shape
    columns = q_all.shape[1]
    heads = columns // length
    share = length // tensors
    tile = NH * length
    scale = HD ** (-0.5)
    factor = scale * LOG2E

    def holder(at):
        return lax.rem(at + y, 2) == 0

    place = (y, x, z, holder)
    other = rank_of(1 - y, NX - 1 - x, NZ - 1 - z)
    peers = [lax.rem(tensor + step, tensors) for step in range(1, tensors)]
    my_rows = pl.ds(pl.multiple_of(tensor * share, share), share)

    loads = [
        pltpu.make_async_copy(source, target, local_sem.at[i])
        for i, (source, target) in enumerate(
            ((x_hbm, x_buf), (wk_hbm, wk), (wv_hbm, wv), (g_hbm, g_all.at[my_rows]), (wq_hbm, wq),
             (wo_hbm, wo))
        )
    ]
    for copy in loads:
        copy.start()
    barrier = pltpu.get_barrier_semaphore()
    ranks = [rank_of(1 - y, x, z), rank_of(y, x, turn(z, 1, NZ)), rank_of(y, x, turn(z, -1, NZ))]
    ranks += [rank_of(y, turn(x, step, NX), z) for step in (1, 2, 3)]
    ranks += [other]
    for who in [{"context": at} for at in ranks] + [{"tensor": at} for at in peers]:
        pl.semaphore_signal(barrier, inc=1, device_id=who, device_id_type=pl.DeviceIdType.MESH)

    cosines, sines = cos_ref[...], sin_ref[...]

    def spread(table):
        return jnp.concatenate([table] * heads, axis=0)

    def swap(field):
        return jnp.concatenate([field[:, HD // 2 :], field[:, : HD // 2]], axis=1)

    def rot(field, cosine_part, sine_part):
        return field * cosine_part + swap(field) * sine_part

    def stack(field):
        return jnp.concatenate([field[:, h * HD : (h + 1) * HD] for h in range(heads)], axis=0)

    def unstack(field):
        return jnp.concatenate(
            [field[h * length : (h + 1) * length] for h in range(heads)], axis=1
        )

    for copy in loads[:3]:
        copy.wait()
    inputs = x_buf[...]
    k_own[...] = rot(matmul(inputs, wk[...], 1, 0), cosines, sines).astype(BF16)
    v_own[...] = (
        mix_ref[0, 0] * matmul(inputs, wv[...], 1, 0) + mix_ref[1, 0] * first_ref[...].astype(F32)
    ).astype(BF16)
    pl.semaphore_wait(barrier, len(ranks) + len(peers))

    send = Sender()
    gather = gather_steps(send, place, k_own, v_own, k_all, v_all, gather_sems)
    next(gather)
    loads[3].wait()
    g_copies = [
        send.go(
            send.build(
                g_all.at[my_rows], g_all.at[my_rows], g_send.at[i], g_recv.at[i], "tensor", peer
            )
        )
        for i, peer in enumerate(peers)
    ]
    next(gather)
    loads[4].wait()
    q_all[y] = rot(
        stack(matmul(x_buf[...], wq[...], 1, 0)), spread(cosines), spread(sines)
    ).astype(BF16)
    pair_q = send.go(
        send.build(q_all.at[y], q_all.at[y], pair_send.at[0], pair_recv.at[0], "context", other)
    )
    next(gather)
    for copy in g_copies:
        copy.wait_recv()
    loads[5].wait()
    for h in range(heads):
        cot_all[y, :, h * length : (h + 1) * length] = matmul(
            wo[h * HD : (h + 1) * HD, :], g_all[...], 1, 1
        ).astype(BF16)
    pair_cot = send.go(
        send.build(cot_all.at[y], cot_all.at[y], pair_send.at[1], pair_recv.at[1], "context", other)
    )
    next(gather)
    xt[...] = x_buf[...].T
    dk_all[...] = jnp.zeros(dk_all.shape, BF16)
    dv_all[...] = jnp.zeros(dv_all.shape, BF16)
    next(gather)
    pair_q.wait_recv()
    pair_cot.wait_recv()

    key_in_tile = lax.broadcasted_iota(jnp.int32, (tile, columns), 0)
    key_in_tile = (2 * (key_in_tile // length) + y) * length + lax.rem(key_in_tile, length)
    query_in_block = lax.rem(lax.broadcasted_iota(jnp.int32, (tile, columns), 1), length)
    low_rank = jnp.minimum(rank, NY * NX * NZ - 1 - rank)

    def block_of(slot):
        return jnp.where(slot == 0, low_rank, NY * NX * NZ - 1 - low_rank)

    def tile_of(ref, row):
        return ref[row // NX, lax.rem(row, NX)].reshape(tile, HD)

    @pl.loop(0, 2)
    def _(slot):
        block = block_of(slot)
        last = block // NZ
        visible = key_in_tile <= query_in_block + lax.rem(block, NZ) * length
        queries = q_all[slot]

        def scores(row):
            return matmul(tile_of(k_all, row), queries, 1, 1)

        def max_step(row, current):
            return jnp.maximum(current, jnp.max(scores(row), axis=0, keepdims=True))

        top = jnp.max(jnp.where(visible, scores(last), NEGATIVE), axis=0, keepdims=True)
        top = lax.fori_loop(0, last, max_step, top) * factor

        def weigh(row, current, masked):
            totals, output = current
            exponent = scores(row) * factor - top
            if masked:
                exponent = jnp.where(visible, exponent, NEGATIVE)
            weight = jnp.exp2(exponent)
            totals = totals + jnp.sum(weight, axis=0, keepdims=True)
            low = weight.astype(BF16)
            weights[slot * NX + row] = low
            return totals, output + matmul(tile_of(v_all, row), low, 0, 0)

        start = (jnp.zeros((1, columns), F32), jnp.zeros((HD, columns), F32))
        start = weigh(last, start, True)
        totals, output = lax.fori_loop(
            0, last, lambda row, current: weigh(row, current, False), start
        )
        delta = jnp.sum(cot_all[slot].astype(F32) * output, axis=0, keepdims=True)
        stat_mine[slot, 0:1] = top
        stat_mine[slot, 1:2] = totals
        stat_mine[slot, 2:3] = delta
        o_acc[slot] = output

    pair_stat = send.go(
        send.build(stat_mine, stat_pair, pair_send.at[2], pair_recv.at[2], "context", other)
    )
    o_send[...] = o_acc[1 - y].astype(BF16)
    pair_o = send.go(
        send.build(o_send, o_recv, pair_send.at[3], pair_recv.at[3], "context", other)
    )
    pair_stat.wait_recv()

    def merged(slot):
        top = jnp.maximum(stat_mine[slot, 0:1], stat_pair[slot, 0:1])
        mine = jnp.exp2(stat_mine[slot, 0:1] - top)
        theirs = jnp.exp2(stat_pair[slot, 0:1] - top)
        inverse = 1.0 / (stat_mine[slot, 1:2] * mine + stat_pair[slot, 1:2] * theirs)
        return mine * inverse, theirs * inverse

    @pl.loop(0, 2)
    def _(step):
        slot = 1 - step
        mine, theirs = merged(slot)
        delta = (stat_mine[slot, 2:3] * mine + stat_pair[slot, 2:3] * theirs) * mine
        scaled = cot_all[slot].astype(F32) * mine
        scaled_across = scaled.astype(BF16)
        scaled_rows = scaled.T.astype(BF16)
        queries = q_all[slot]

        def back(row, query_grad):
            low = weights[slot * NX + row]
            change = matmul(tile_of(v_all, row), scaled_across, 1, 0) - delta
            score_grad = (low.astype(F32) * change).astype(BF16)
            key_term = matmul(score_grad, queries, 1, 0) * scale
            value_term = matmul(low, scaled_rows, 1, 0)
            shape = (NH, length, HD)
            at = (row // NX, lax.rem(row, NX))
            dk_all[at] = (dk_all[at].astype(F32) + key_term.reshape(shape)).astype(BF16)
            dv_all[at] = (dv_all[at].astype(F32) + value_term.reshape(shape)).astype(BF16)
            return query_grad + matmul(tile_of(k_all, row), score_grad, 0, 0)

        dq_acc[slot] = lax.fori_loop(
            0, block_of(slot) // NZ + 1, back, jnp.zeros((HD, columns), F32)
        )

    scatter = scatter_steps(
        send, place, True, dk_all, dv_all, k_sum, v_sum, grad_bufs, grad_sems
    )
    next(scatter)
    dq_send[...] = dq_acc[1 - y].astype(BF16)
    pair_dq = send.go(
        send.build(dq_send, dq_recv, pair_send.at[4], pair_recv.at[4], "context", other)
    )

    def share_out(part, recv, send_sem, recv_sem):
        return [
            send.go(
                send.build(
                    part.at[peer], recv.at[i], send_sem.at[i], recv_sem.at[i], "tensor", peer
                )
            )
            for i, peer in enumerate(peers)
        ]

    def add_up(part, recv, copies, out):
        for copy in copies:
            copy.wait_recv()
        summed = part[tensor].astype(F32)
        for i in range(len(copies)):
            summed = summed + recv[i].astype(F32)
        out[...] = summed.astype(BF16)

    strip = min(512, width)

    def strip_of(index):
        return pl.ds(pl.multiple_of(index * strip, strip), strip)

    pair_o.wait_recv()
    mine, theirs = merged(y)
    outputs = unstack(
        (o_acc[y] * mine + o_recv[...].astype(F32) * theirs).T.astype(BF16)
    )

    @pl.loop(0, width // strip)
    def _(index):
        at = strip_of(index)
        term = matmul(outputs, wo[:, at], 1, 0).astype(BF16)
        for peer in range(tensors):
            part_out[peer, :, at] = term[peer * share : (peer + 1) * share]

    out_copies = share_out(part_out, recv_out, out_send, out_recv)
    next(scatter)
    pair_dq.wait_recv()
    query_pre = unstack(
        rot(
            (dq_acc[y] + dq_recv[...].astype(F32)).T * scale, spread(cosines), -spread(sines)
        ).astype(BF16)
    )

    @pl.loop(0, width // strip)
    def _(index):
        at = strip_of(index)
        acc_in[:, at] = matmul(query_pre, wq[at, :], 1, 1)

    next(scatter)
    next(scatter)
    add_up(part_out, recv_out, out_copies, attn_ref)
    next(scatter)
    key_pre = rot(k_sum[...], cosines, -sines).astype(BF16)
    value_sum = v_sum[...]
    value_pre = (mix_ref[0, 0] * value_sum).astype(BF16)
    strips = wk_part.shape
    wk_part[...] = matmul(xt[...], key_pre, 1, 0).astype(BF16).reshape(strips)
    wv_part[...] = matmul(xt[...], value_pre, 1, 0).astype(BF16).reshape(strips)
    scatter = scatter_steps(
        send, place, False, wk_part, wv_part, gwk_ref, gwv_ref, weight_bufs, weight_sems
    )
    next(scatter)
    gfirst_ref[...] = (mix_ref[1, 0] * value_sum).astype(BF16)

    @pl.loop(0, width // strip)
    def _(index):
        at = strip_of(index)
        term = acc_in[:, at] + matmul(key_pre, wk[at, :], 1, 1)
        term = (term + matmul(value_pre, wv[at, :], 1, 1)).astype(BF16)
        for peer in range(tensors):
            part_in[peer, :, at] = term[peer * share : (peer + 1) * share]

    in_copies = share_out(part_in, recv_in, in_send, in_recv)
    for _ in range(3):
        next(scatter)
    add_up(part_in, recv_in, in_copies, gin_ref)
    next(scatter)
    send.finish()


def rope_tables(positions, head_width):
    half_width = head_width // 2
    exponent = jnp.arange(half_width, dtype=F32) * (2.0 / head_width)
    frequency = jnp.power(jnp.float32(THETA), -exponent)
    angles = positions.astype(F32)[:, None] * frequency[None, :]
    return (jnp.cos(angles), jnp.sin(angles))


def shards(hidden_in, value_first, w_query, w_key, w_value, w_out, value_mix, grad_out):
    tensors = lax.axis_size("tensor")
    length, width = hidden_in.shape[1:]
    features = w_query.shape[1]
    columns = features // HD * length
    share = length // tensors
    rows = width // (NY * NX * NZ)
    block_rows = lax.axis_index("context") * length + jnp.arange(length, dtype=jnp.int32)
    cosines, sines = rope_tables(block_rows, HD)
    cosines = jnp.concatenate([cosines, cosines], axis=1)
    sines = jnp.concatenate([-sines, sines], axis=1)
    vmem = pl.BlockSpec(memory_space=pltpu.VMEM)
    hbm = pl.BlockSpec(memory_space=pl.ANY)
    smem = pl.BlockSpec(memory_space=pltpu.SMEM)
    dma = pltpu.SemaphoreType.DMA

    def low(*shape):
        return pltpu.VMEM(shape, BF16)

    def full(*shape):
        return pltpu.VMEM(shape, F32)

    def scatter_room(ends, count):
        return (
            low(4, 4, NX, count, HD), low(4, 2, ends, count, HD), low(4, 4, count, HD),
            low(NX, NY, count, HD), low(NY, ends, count, HD), low(3, NY, count, HD),
            low(2, NY, count, HD), low(2, count, HD),
        )

    others = (max(tensors - 1, 1),)
    scratch = [
        low(length, width), low(width, features), low(width, HD), low(width, HD),
        low(features, width), low(length, width), low(width, length), low(length, HD),
        low(length, HD), low(NY, NX, NH, length, HD), low(NY, NX, NH, length, HD),
        low(2, columns, HD), low(2, HD, columns), low(3 * NX, NH * length, columns),
        full(2, HD, columns), full(2, HD, columns), low(HD, columns), low(HD, columns),
        low(HD, columns), low(HD, columns), full(2, 8, columns), full(2, 8, columns),
        low(NY, NX, NH, length, HD), low(NY, NX, NH, length, HD), full(length, HD),
        full(length, HD), low(tensors, share, width), low(others[0], share, width),
        low(tensors, share, width), low(others[0], share, width), full(length, width),
        low(NY, NX, NZ, rows, HD), low(NY, NX, NZ, rows, HD),
        scatter_room(NH, length), scatter_room(NZ, rows), dma((6,)),
        (dma((2,)), dma((2,)), dma((3,)), dma((3,)), dma((4, 4)), dma((4, 4)), dma((4, 4)),
         dma((4, 4)), dma((4, 2)), dma((4, 2))),
    ]
    scatter_sems = (
        dma((4, 4)), dma((4, 4)), dma((4, 2)), dma((4, 2)), dma((4, 4)), dma((4, 4)), dma((3,)),
        dma((3,)), dma((2,)), dma((2,)),
    )
    scratch += [scatter_sems, scatter_sems, dma((5,)), dma((5,))] + [dma(others)] * 6
    attn_out, grad_in, grad_first, key_weight, value_weight = pl.pallas_call(
        block_kernel,
        out_shape=(
            jax.ShapeDtypeStruct((share, width), BF16),
            jax.ShapeDtypeStruct((share, width), BF16),
            jax.ShapeDtypeStruct((length, HD), BF16),
            jax.ShapeDtypeStruct((rows, HD), F32),
            jax.ShapeDtypeStruct((rows, HD), F32),
        ),
        in_specs=[hbm, vmem, hbm, hbm, hbm, hbm, smem, hbm, vmem, vmem],
        out_specs=(vmem,) * 5,
        scratch_shapes=scratch,
        compiler_params=pltpu.CompilerParams(
            collective_id=1, has_side_effects=True, vmem_limit_bytes=56 * 2**20
        ),
        name="attention_block",
    )(
        hidden_in.reshape(length, width), value_first.reshape(length, HD), w_query, w_key, w_value,
        w_out, value_mix, grad_out.reshape(share, width), cosines, sines,
    )
    return (
        attn_out.reshape(1, share, width),
        grad_in.reshape(1, share, width),
        grad_first.reshape(1, length, HD),
        key_weight,
        value_weight,
    )


def solution(mesh):
    return jax.shard_map(
        shards,
        mesh=mesh,
        in_specs=(
            P("context", None, None),
            P("context", None, "tensor"),
            P(None, "tensor"),
            P(None, "tensor"),
            P(None, "tensor"),
            P("tensor", None),
            P(None, "tensor"),
            P("context", "tensor", None),
        ),
        out_specs=(
            P("context", "tensor", None),
            P("context", "tensor", None),
            P("context", None, "tensor"),
            P("context", "tensor"),
            P("context", "tensor"),
        ),
        check_vma=False,
    )
```

time: 2280 us -> 144 us (0.06); the launches traced: 2240 us -> 142 us
  waiting for transfers between devices: 1250 us -> 0 us
  local copies, waits for them, and re-layouts: 452 us -> 8.76 us
  other arithmetic: 252 us -> 1.08 us
  loops' own time: 238 us -> 0 us
  Pallas kernels: 0 us -> 131 us
  matrix products: 34.8 us -> 0 us
    reduce_scatter x3 -> x0, waiting for transfers between devices: 786 us -> none  [the longest x1 737 us: shards(): lax.psum_scatter(key_terms.reshape(context_count * length, 2 * kv_width),...]
    unnamed x8 -> x0, waiting for transfers between devices: 353 us -> none
    dynamic_update_slice x64 -> x0, local copies, waits for them, and re-layouts: 300 us -> none  [shards(): lax.scan(back_block, jnp.zeros((local_kv, group_size, length, head_width)...]
    add x195 -> x0, other arithmetic: 247 us -> none  [the longest x64 83.8 us: stats_block(): key_positions = first_row + jnp.arange(key_block.shape[0], dtype=jnp.int32)]
    another operation x195 -> x0, loops' own time: 238 us -> none  [the longest x2 156 us: over_blocks(): return lax.scan(step_block, running, block_items)[0]]
    pallas_call x0 -> x1, Pallas kernels: none -> 131 us  [shards(): pl.pallas_call(block_kernel, out_shape=(jax.ShapeDtypeStruct((share, widt...]
    dynamic_slice x192 -> x0, local copies, waits for them, and re-layouts: 112 us -> none  [over_blocks(): return lax.scan(step_block, running, block_items)[0]]
    all_gather x3 -> x0, waiting for transfers between devices: 111 us -> none  [the longest x1 100 us: shards(): lax.all_gather(keys_here, 'context', axis=0, tiled=True)]
  transfers between devices with their start and end apart: 7 -> 0, of which waited for: 6 -> 0; matrix products, arithmetic and copies ran while one was open for 7% -> 0% of each run, Pallas kernels for 0% -> 0%
where the time goes in v2:
time: 144 us; the launch traced here: 142 us
  Pallas kernels  131 us (91%)
  local copies, waits for them, and re-layouts  8.76 us (6%)
    pallas_call x1, Pallas kernels, shards(): pl.pallas_call(block_kernel, out_shape=(jax.ShapeDtypeStruct((share, widt...  131 us
    unnamed x6, local copies, waits for them, and re-layouts  8.76 us

profile of v2, /device:TPU:32, one launch (start us, length us, event | category | flops | bytes accessed | tf_op | source)
XLA Modules:
  0.0 141.9 jit_solution(12447570510972325933)
XLA Ops:
  0.7 1.3 copy.13.mix_ref
  2.0 0.3 fusion
  2.3 0.8 pad_maximum_fusion
  3.0 131.4 %attention_block.1 = (bf16[32,4096]{1,0:T(8,128)(2,1)}, bf16[32,4096]{1,0:T(8,128)(2,1)}, bf16[128,128]{1,0:T(8,128)(2,1)}, f32[64,128]{1,0:T(8,128)}, f32[64,128]{1,0:T(8,128)}) custom-call(bf16[128,4096]{1,0:T(8,128)(2,1)} %bitcast.6, bf16[128,128]{1,0:T(8,128)(2,1)} %bitcast.10, bf16[4096,512]{1,0:T(8,128)(2,1)} %wq_hbm.1, bf16[4096,128]{1,0:T(8,128)(2,1)} %wk_hbm.1, ...), custom_call_target="tpu_custom_call" | custom-call | tf_op jit(solution)/shard_map/attention_block/pallas_call | solution.py:689
  134.5 1.7 %copy.19 = bf16[1,32,4096]{2,1,0:T(8,128)(2,1)} copy(bf16[1,32,4096]{2,1,0:T(8,128)(2,1)} %bitcast.9) | data formatting | bytes 524288
  136.2 1.7 %copy.20 = bf16[1,32,4096]{2,1,0:T(8,128)(2,1)} copy(bf16[1,32,4096]{2,1,0:T(8,128)(2,1)} %bitcast.8) | data formatting | bytes 524288
  137.8 1.4 copy.21
  139.2 1.4 copy.22
  140.6 1.4 copy.23
  (2 shorter events, 0.0 us)

commit v3 on v2

v3 whole, which is shorter than its diff:
```python
import jax
import jax.numpy as jnp
from jax import lax
from jax.experimental import pallas as pl
from jax.experimental.pallas import tpu as pltpu
from jax.sharding import PartitionSpec as P

HD = 128
THETA = 500000.0
LOG2E = 1.4426950408889634
NEGATIVE = -1e30
NY, NX, NZ = 2, 4, 8
NH = NZ // 2
F32, BF16 = jnp.float32, jnp.bfloat16

CHAINS = ((1, 0, 4, 2), (1, 1, 3, 1), (-1, 1, 4, 2), (-1, 0, 3, 1))
ORDER = (0, 2, 1, 3)
ARRIVE = ((0, 3), (1, 2))


def rank_of(y, x, z):
    return (y * NX + x) * NZ + z


def turn(value, step, count):
    return lax.rem(value + (step + count), count)


def when(condition, action):
    if condition is True:
        action()
    else:
        pl.when(condition)(action)


def matmul(left, right, left_dim, right_dim):
    return lax.dot_general(
        left, right, (((left_dim,), (right_dim,)), ((), ())), preferred_element_type=F32
    )


def add_into(target, term):
    target[...] = (target[...].astype(F32) + term[...].astype(F32)).astype(BF16)


class Sender:
    def __init__(self):
        self.started = []

    def build(self, source, target, send_sem, recv_sem, axis, rank):
        return pltpu.make_async_remote_copy(
            src_ref=source,
            dst_ref=target,
            send_sem=send_sem,
            recv_sem=recv_sem,
            device_id={axis: rank},
            device_id_type=pl.DeviceIdType.MESH,
        )

    def go(self, copy, condition=True):
        copy.start()
        self.started.append((condition, copy))
        return copy

    def finish(self):
        for condition, copy in self.started:
            when(condition, copy.wait_send)


def gather_steps(send, place, k_own, v_own, k_all, v_all, sems):
    y, x, z, holder = place
    y_send, y_recv, kx_send, kx_recv, vz_send, vz_recv, kz_send, kz_recv = sems[:8]
    vx_send, vx_recv, vf_send, vf_recv = sems[8:]
    slot = z // 2
    partner = rank_of(1 - y, x, z)
    lends = jnp.logical_not(holder(z))
    pairs = [
        send.build(own, whole.at[y, x, slot], y_send.at[i], y_recv.at[i], "context", partner)
        for i, (own, whole) in enumerate(((k_own, k_all), (v_own, v_all)))
    ]

    def lend():
        for copy in pairs:
            copy.start()

    def keep():
        k_all[y, x, slot] = k_own[...]
        v_all[y, x, slot] = v_own[...]

    pl.when(lends)(lend)
    pl.when(holder(z))(keep)
    send.started += [(lends, copy) for copy in pairs]

    kx = {}
    for step in (1, 3, 2):
        part = k_all.at[:, x, slot]
        kx[step] = send.build(
            part, part, kx_send.at[step - 1], kx_recv.at[step - 1], "context",
            rank_of(y, turn(x, step, NX), z),
        )
    rows = (0, 1, 3, 2)

    def kz_copy(chain, hop, part_at):
        way, half, _, _ = CHAINS[chain]
        part = k_all.at[half, turn(x, rows[part_at], NX), turn(z, -way * hop, NZ) // 2]
        return send.build(
            part, part, kz_send.at[chain, hop, part_at], kz_recv.at[chain, hop, part_at],
            "context", rank_of(y, x, turn(z, way, NZ)),
        )

    def kz(hop, part_at):
        if hop == 0 and part_at:
            pl.when(holder(z))(kx[NX - rows[part_at]].wait_recv)
        for chain in ORDER:
            if hop < CHAINS[chain][2]:
                condition = holder(turn(z, -CHAINS[chain][0] * hop, NZ))
                copy = kz_copy(chain, hop, part_at)

                def act():
                    if hop:
                        kz_copy(chain, hop - 1, part_at).wait_recv()
                    copy.start()

                when(condition, act)
                send.started.append((condition, copy))

    def vz_copy(chain, hop):
        way, half, _, _ = CHAINS[chain]
        part = v_all.at[half, x, turn(z, -way * hop, NZ) // 2]
        return send.build(
            part, part, vz_send.at[chain, hop], vz_recv.at[chain, hop], "context",
            rank_of(y, x, turn(z, way, NZ)),
        )

    def vx_copy(half, at, way):
        part = v_all.at[half, x, at]
        side = 0 if way > 0 else 1
        return send.build(
            part, part, vx_send.at[half, at, side], vx_recv.at[half, at, side], "context",
            rank_of(y, turn(x, way, NX), z),
        )

    def vf_copy(half, at):
        way = 1 if half == 0 else -1
        part = v_all.at[half, turn(x, -way, NX), at]
        return send.build(
            part, part, vf_send.at[half, at], vf_recv.at[half, at], "context",
            rank_of(y, turn(x, way, NX), z),
        )

    def pieces(distance):
        if distance == 0:
            return [(None, holder(z), half, slot) for half in range(NY)]
        found = []
        for chain in ORDER:
            way, half, hops, _ = CHAINS[chain]
            if distance <= hops:
                origin = turn(z, -way * distance, NZ)
                found.append((chain, holder(origin), half, origin // 2))
        return found

    def v_round(distance):
        for chain, condition, half, at in pieces(distance):
            copies = [vx_copy(half, at, 1), vx_copy(half, at, -1)]
            if chain is None:
                copies += [vz_copy(c, 0) for c in ORDER if CHAINS[c][1] == half]
            elif distance < CHAINS[chain][2]:
                copies.insert(0, vz_copy(chain, distance))

            def act():
                if chain is not None:
                    vz_copy(chain, distance - 1).wait_recv()
                for copy in copies:
                    copy.start()

            when(condition, act)
            send.started += [(condition, copy) for copy in copies]

    def forward(distance):
        for _, condition, half, at in pieces(distance):
            copy = vf_copy(half, at)

            def act():
                vx_copy(half, at, 1 if half == 0 else -1).wait_recv()
                copy.start()

            when(condition, act)
            send.started.append((condition, copy))

    def finish():
        for distance in range(5):
            for _, condition, half, at in pieces(distance):

                def act():
                    vx_copy(half, at, -1 if half == 0 else 1).wait_recv()
                    vf_copy(half, at).wait_recv()

                when(condition, act)
        for chain in ORDER:
            way, _, hops, _ = CHAINS[chain]
            condition = holder(turn(z, -way * hops, NZ))

            def act():
                for part_at in range(NX):
                    kz_copy(chain, hops - 1, part_at).wait_recv()

            when(condition, act)

    yield

    def start_rows():
        for copy in pairs:
            copy.wait_recv()
        for copy in kx.values():
            copy.start()

    pl.when(holder(z))(start_rows)
    send.started += [(holder(z), copy) for copy in kx.values()]
    v_round(0)
    kz(0, 0)
    v_round(1)
    kz(0, 1)
    kz(1, 0)
    forward(0)
    yield
    v_round(2)
    kz(0, 2)
    kz(1, 1)
    kz(2, 0)
    forward(1)
    yield
    v_round(3)
    kz(0, 3)
    kz(1, 2)
    kz(2, 1)
    kz(3, 0)
    forward(2)
    v_round(4)
    kz(1, 3)
    kz(2, 2)
    kz(3, 1)
    forward(3)
    kz(2, 3)
    kz(3, 2)
    forward(4)
    kz(3, 3)
    yield
    finish()
    yield


def fold_steps(send, place, parity, a_in, b_in, a_out, b_out, bufs, sems):
    y, x, z, holder_of = place

    def holder(at):
        return holder_of(at) if parity else True

    def index(at):
        return at // 2 if parity else at

    az_buf, far_buf, near_buf, bz_buf, a_sum, b_sum, ax_buf, low, y_buf = bufs
    az_send, az_recv, far_send, far_recv, near_send, near_recv, bz_send, bz_recv = sems[:8]
    ax_send, ax_recv, y_send, y_recv = sems[8:]
    slot = index(z)
    rows = (2, 1, 3, 0)

    def az_copy(chain, hop, part_at):
        way, half, hops, _ = CHAINS[chain]
        own = a_in.at[half, turn(x, rows[part_at], NX), index(turn(z, way * (hops - hop), NZ))]
        source = az_buf.at[chain, hop - 1, part_at] if hop else own
        copy = send.build(
            source, az_buf.at[chain, hop, part_at], az_send.at[chain, hop, part_at],
            az_recv.at[chain, hop, part_at], "context", rank_of(y, x, turn(z, way, NZ)),
        )
        return own, copy

    def az(hop, part_at):
        for chain in ORDER:
            way, _, hops, _ = CHAINS[chain]
            if hop < hops:
                condition = holder(turn(z, way * (hops - hop), NZ))
                own, copy = az_copy(chain, hop, part_at)

                def act():
                    if hop:
                        az_copy(chain, hop - 1, part_at)[1].wait_recv()
                        add_into(az_buf.at[chain, hop - 1, part_at], own)
                    copy.start()

                when(condition, act)
                send.started.append((condition, copy))

    def ax_copy(step):
        goal = turn(x, step, NX)
        return send.build(
            a_sum.at[goal], ax_buf.at[step - 1], ax_send.at[step - 1], ax_recv.at[step - 1],
            "context", rank_of(y, goal, z),
        )

    def a_end(part_at):
        row = turn(x, rows[part_at], NX)

        def act():
            for half in range(NY):
                summed = a_in[half, row, slot].astype(F32)
                for chain in ARRIVE[half]:
                    hops = CHAINS[chain][2]
                    az_copy(chain, hops - 1, part_at)[1].wait_recv()
                    summed = summed + az_buf[chain, hops - 1, part_at].astype(F32)
                a_sum[row, half] = summed.astype(BF16)
            if rows[part_at]:
                ax_copy(rows[part_at]).start()

        when(holder(z), act)
        if rows[part_at]:
            send.started.append((holder(z), ax_copy(rows[part_at])))

    def pieces(distance):
        if distance == 0:
            return [(None, holder(z), half, slot) for half in range(NY)]
        found = []
        for chain in ORDER:
            way, half, hops, _ = CHAINS[chain]
            if distance <= hops:
                goal = turn(z, way * distance, NZ)
                found.append((chain, holder(goal), half, index(goal)))
        return found

    def outward(half):
        return 1 if half == 0 else -1

    def far_copy(half, at):
        way = outward(half)
        return send.build(
            b_in.at[half, turn(x, 2, NX), at], far_buf.at[half, at], far_send.at[half, at],
            far_recv.at[half, at], "context", rank_of(y, turn(x, way, NX), z),
        )

    def near_copy(half, at, way):
        side = 0 if way > 0 else 1
        goal = turn(x, way, NX)
        source = far_buf.at[half, at] if way == outward(half) else b_in.at[half, goal, at]
        return send.build(
            source, near_buf.at[half, at, side], near_send.at[half, at, side],
            near_recv.at[half, at, side], "context", rank_of(y, goal, z),
        )

    def b_start(distance):
        for _, condition, half, at in pieces(distance):
            copies = [far_copy(half, at), near_copy(half, at, -outward(half))]

            def act():
                for copy in copies:
                    copy.start()

            when(condition, act)
            send.started += [(condition, copy) for copy in copies]

    def b_middle(distance):
        for _, condition, half, at in pieces(distance):
            copy = near_copy(half, at, outward(half))

            def act():
                far_copy(half, at).wait_recv()
                add_into(far_buf.at[half, at], b_in.at[half, turn(x, outward(half), NX), at])
                copy.start()

            when(condition, act)
            send.started.append((condition, copy))

    def bz_copy(chain, hop):
        way, half, hops, _ = CHAINS[chain]
        own = b_sum.at[half, index(turn(z, way * (hops - hop), NZ))]
        return send.build(
            own, bz_buf.at[chain, hop], bz_send.at[chain, hop], bz_recv.at[chain, hop],
            "context", rank_of(y, x, turn(z, way, NZ)),
        )

    def b_end(distance):
        for chain, condition, half, at in pieces(distance):
            if chain is not None:
                hop = CHAINS[chain][2] - distance

            def act():
                summed = b_in[half, x, at].astype(F32)
                for way in (1, -1):
                    near_copy(half, at, way).wait_recv()
                    summed = summed + near_buf[half, at, 0 if way > 0 else 1].astype(F32)
                if chain is None:
                    arrivals = [(c, CHAINS[c][2] - 1) for c in ARRIVE[half]]
                else:
                    arrivals = [(chain, hop - 1)] if hop else []
                for other, at_hop in arrivals:
                    bz_copy(other, at_hop).wait_recv()
                    summed = summed + bz_buf[other, at_hop].astype(F32)
                if chain is None:
                    low[1, half] = summed.astype(BF16)
                else:
                    b_sum[half, at] = summed.astype(BF16)
                    bz_copy(chain, hop).start()

            when(condition, act)
            if chain is not None:
                send.started.append((condition, bz_copy(chain, hop)))

    partner = rank_of(1 - y, x, z)
    pairs = [
        send.build(
            low.at[i, 1 - y], y_buf.at[i], y_send.at[i], y_recv.at[i], "context", partner
        )
        for i in range(2)
    ]

    def hand_over(i):
        when(holder(z), pairs[i].start)
        send.started.append((holder(z), pairs[i]))

    def close(i, out):
        def keep():
            out[...] = low[i, y].astype(F32)

        def take():
            pairs[i].wait_recv()
            out[...] = y_buf[i].astype(F32)

        if parity:
            pl.when(holder(z))(keep)
            pl.when(jnp.logical_not(holder(z)))(take)
        else:
            pairs[i].wait_recv()
            out[...] = low[i, y].astype(F32) + y_buf[i].astype(F32)

    def a_row():
        for step in (1, 2, 3):
            ax_copy(step).wait_recv()
        summed = a_sum[x].astype(F32)
        for step in range(3):
            summed = summed + ax_buf[step].astype(F32)
        low[0] = summed.astype(BF16)

    b_start(4)
    b_start(3)
    az(0, 0)
    az(0, 1)
    b_start(2)
    az(0, 2)
    b_start(1)
    az(0, 3)
    b_start(0)
    yield
    b_middle(4)
    b_middle(3)
    az(1, 0)
    az(1, 1)
    b_middle(2)
    b_end(4)
    b_end(3)
    yield
    az(1, 2)
    az(2, 0)
    b_middle(1)
    az(1, 3)
    az(2, 1)
    b_middle(0)
    b_end(2)
    az(3, 0)
    az(2, 2)
    az(3, 1)
    b_end(1)
    a_end(0)
    yield
    az(2, 3)
    az(3, 2)
    a_end(1)
    az(3, 3)
    a_end(2)
    b_end(0)
    hand_over(1)
    a_end(3)
    when(holder(z), a_row)
    hand_over(0)
    close(1, b_out)
    close(0, a_out)
    yield


def block_kernel(
    x_hbm, first_ref, wq_hbm, wk_hbm, wv_hbm, wo_hbm, g_hbm, table_ref,
    attn_ref, gin_ref, gfirst_ref, gwk_ref, gwv_ref,
    x_buf, wq, wkv, wo, g_all, xt, k_own, v_own, k_all, v_all, q_all, cot_all, weights,
    o_acc, dq_acc, o_send, o_recv, dq_send, dq_recv, stat_mine, stat_pair, dk_all, dv_all,
    k_sum, v_sum, part_out, recv_out, part_in, recv_in, acc_in, xt_far,
    pre_own, pre_far, w_part, w_far, w_low, w_last, grad_bufs, local_sem, gather_sems, grad_sems,
    row_send, row_recv, ring_send, ring_recv,
    pair_send, pair_recv, g_send, g_recv, out_send, out_recv, in_send, in_recv,
):
    rank = lax.axis_index("context")
    y, x, z = rank // (NX * NZ), (rank // NZ) % NX, rank % NZ
    tensor, tensors = lax.axis_index("tensor"), lax.axis_size("tensor")
    length, width = x_buf.shape
    columns = q_all.shape[1]
    heads = columns // length
    share = length // tensors
    tile = NH * length
    scale = HD ** (-0.5)
    factor = scale * LOG2E

    def holder(at):
        return lax.rem(at + y, 2) == 0

    place = (y, x, z, holder)
    other = rank_of(1 - y, NX - 1 - x, z)
    peers = [lax.rem(tensor + step, tensors) for step in range(1, tensors)]
    my_rows = pl.ds(pl.multiple_of(tensor * share, share), share)

    loads = [
        pltpu.make_async_copy(source, target, local_sem.at[i])
        for i, (source, target) in enumerate(
            ((x_hbm, x_buf), (wk_hbm, wkv.at[:, :HD]), (wv_hbm, wkv.at[:, HD:]), (g_hbm, g_all.at[my_rows]), (wq_hbm, wq),
             (wo_hbm, wo))
        )
    ]
    for copy in loads:
        copy.start()
    barrier = pltpu.get_barrier_semaphore()
    ranks = [rank_of(1 - y, x, z), rank_of(y, x, turn(z, 1, NZ)), rank_of(y, x, turn(z, -1, NZ))]
    ranks += [rank_of(y, turn(x, step, NX), z) for step in (1, 2, 3)]
    ranks += [rank_of(y, x, turn(z, step, NZ)) for step in range(2, NZ - 1)]
    ranks += [other]
    for who in [{"context": at} for at in ranks] + [{"tensor": at} for at in peers]:
        pl.semaphore_signal(barrier, inc=1, device_id=who, device_id_type=pl.DeviceIdType.MESH)

    cosines, sines = table_ref[:length], table_ref[length : 2 * length]
    mix_here = table_ref[2 * length : 2 * length + 1]
    mix_first = table_ref[2 * length + 1 : 2 * length + 2]

    def spread(table):
        return jnp.concatenate([table] * heads, axis=0)

    def swap(field):
        return jnp.concatenate([field[:, HD // 2 :], field[:, : HD // 2]], axis=1)

    def rot(field, cosine_part, sine_part):
        return field * cosine_part + swap(field) * sine_part

    def stack(field):
        return jnp.concatenate([field[:, h * HD : (h + 1) * HD] for h in range(heads)], axis=0)

    def unstack(field):
        return jnp.concatenate(
            [field[h * length : (h + 1) * length] for h in range(heads)], axis=1
        )

    for copy in loads[:3]:
        copy.wait()
    projected = matmul(x_buf[...], wkv[...], 1, 0)
    k_own[...] = rot(projected[:, :HD], cosines, sines).astype(BF16)
    v_own[...] = (
        mix_here * projected[:, HD:] + mix_first * first_ref[...].astype(F32)
    ).astype(BF16)
    pl.semaphore_wait(barrier, len(ranks) + len(peers))

    send = Sender()
    gather = gather_steps(send, place, k_own, v_own, k_all, v_all, gather_sems)
    next(gather)
    loads[3].wait()
    g_copies = [
        send.go(
            send.build(
                g_all.at[my_rows], g_all.at[my_rows], g_send.at[i], g_recv.at[i], "tensor", peer
            )
        )
        for i, peer in enumerate(peers)
    ]
    loads[4].wait()
    q_all[y] = rot(
        stack(matmul(x_buf[...], wq[...], 1, 0)), spread(cosines), spread(sines)
    ).astype(BF16)
    pair_q = send.go(
        send.build(q_all.at[y], q_all.at[y], pair_send.at[0], pair_recv.at[0], "context", other)
    )
    for _ in range(3):
        next(gather)
    for copy in g_copies:
        copy.wait_recv()
    loads[5].wait()
    for h in range(heads):
        cot_all[y, :, h * length : (h + 1) * length] = matmul(
            wo[h * HD : (h + 1) * HD, :], g_all[...], 1, 1
        ).astype(BF16)
    pair_cot = send.go(
        send.build(cot_all.at[y], cot_all.at[y], pair_send.at[1], pair_recv.at[1], "context", other)
    )
    xt[...] = x_buf[...].T.reshape(xt.shape)
    next(gather)
    row_x = []
    for step in (1, 3, 2):
        goal = turn(x, step, NX)
        row_x.append(
            send.go(
                send.build(
                    xt.at[:, goal], xt_far.at[step - 1], row_send.at[step - 1],
                    row_recv.at[step - 1], "context", rank_of(y, goal, z),
                )
            )
        )
    pair_q.wait_recv()

    key_in_tile = lax.broadcasted_iota(jnp.int32, (tile, columns), 0)
    key_in_tile = (2 * (key_in_tile // length) + y) * length + lax.rem(key_in_tile, length)
    query_in_block = lax.rem(lax.broadcasted_iota(jnp.int32, (tile, columns), 1), length)
    def row_of(slot):
        return jnp.where(slot == y, y * NX + x, slot * NX + NX - 1 - x)

    def tile_of(ref, row):
        return ref[row // NX, lax.rem(row, NX)].reshape(tile, HD)

    @pl.loop(0, 2)
    def _(slot):
        last = row_of(slot)
        visible = key_in_tile <= query_in_block + z * length
        queries = q_all[slot].astype(F32).T.astype(BF16)

        def scores(row):
            return matmul(tile_of(k_all, row), queries, 1, 0)

        def max_step(row, current):
            return jnp.maximum(current, jnp.max(scores(row), axis=0, keepdims=True))

        top = jnp.max(jnp.where(visible, scores(last), NEGATIVE), axis=0, keepdims=True)
        top = lax.fori_loop(0, last, max_step, top) * factor

        def weigh(row, current, masked):
            totals, output = current
            exponent = scores(row) * factor - top
            if masked:
                exponent = jnp.where(visible, exponent, NEGATIVE)
            weight = jnp.exp2(exponent)
            totals = totals + jnp.sum(weight, axis=0, keepdims=True)
            low = weight.astype(BF16)
            weights[slot * NX + row] = low
            return totals, output + matmul(tile_of(v_all, row), low, 0, 0)

        start = (jnp.zeros((1, columns), F32), jnp.zeros((HD, columns), F32))
        start = weigh(last, start, True)
        totals, output = lax.fori_loop(
            0, last, lambda row, current: weigh(row, current, False), start
        )
        stat_mine[slot, 0:1] = top
        stat_mine[slot, 1:2] = totals
        o_acc[slot] = output

    pair_cot.wait_recv()
    for slot in range(2):
        stat_mine[slot, 2:3] = jnp.sum(
            cot_all[slot].astype(F32) * o_acc[slot], axis=0, keepdims=True
        )
    pair_stat = send.go(
        send.build(stat_mine, stat_pair, pair_send.at[2], pair_recv.at[2], "context", other)
    )
    o_send[...] = o_acc[1 - y].astype(BF16)
    pair_o = send.go(
        send.build(o_send, o_recv, pair_send.at[3], pair_recv.at[3], "context", other)
    )
    dk_all[...] = jnp.zeros(dk_all.shape, BF16)
    dv_all[...] = jnp.zeros(dv_all.shape, BF16)
    pair_stat.wait_recv()

    def merged(slot):
        top = jnp.maximum(stat_mine[slot, 0:1], stat_pair[slot, 0:1])
        mine = jnp.exp2(stat_mine[slot, 0:1] - top)
        theirs = jnp.exp2(stat_pair[slot, 0:1] - top)
        inverse = 1.0 / (stat_mine[slot, 1:2] * mine + stat_pair[slot, 1:2] * theirs)
        return mine * inverse, theirs * inverse

    @pl.loop(0, 2)
    def _(step):
        slot = 1 - step
        mine, theirs = merged(slot)
        delta = (stat_mine[slot, 2:3] * mine + stat_pair[slot, 2:3] * theirs) * mine
        scaled = cot_all[slot].astype(F32) * mine
        scaled_across = scaled.astype(BF16)
        scaled_rows = scaled.T.astype(BF16)
        queries = q_all[slot]

        def back(row, query_grad):
            low = weights[slot * NX + row]
            change = matmul(tile_of(v_all, row), scaled_across, 1, 0) - delta
            score_grad = (low.astype(F32) * change).astype(BF16)
            key_term = matmul(score_grad, queries, 1, 0) * scale
            value_term = matmul(low, scaled_rows, 1, 0)
            shape = (NH, length, HD)
            at = (row // NX, lax.rem(row, NX))
            dk_all[at] = (dk_all[at].astype(F32) + key_term.reshape(shape)).astype(BF16)
            dv_all[at] = (dv_all[at].astype(F32) + value_term.reshape(shape)).astype(BF16)
            return query_grad + matmul(tile_of(k_all, row), score_grad, 0, 0)

        dq_acc[slot] = lax.fori_loop(
            0, row_of(slot) + 1, back, jnp.zeros((HD, columns), F32)
        )

    scatter = fold_steps(
        send, place, True, dk_all, dv_all, k_sum, v_sum, grad_bufs, grad_sems
    )
    next(scatter)
    dq_send[...] = dq_acc[1 - y].astype(BF16)
    pair_dq = send.go(
        send.build(dq_send, dq_recv, pair_send.at[4], pair_recv.at[4], "context", other)
    )

    def share_out(part, recv, send_sem, recv_sem):
        return [
            send.go(
                send.build(
                    part.at[peer], recv.at[i], send_sem.at[i], recv_sem.at[i], "tensor", peer
                )
            )
            for i, peer in enumerate(peers)
        ]

    def add_up(part, recv, copies, out):
        for copy in copies:
            copy.wait_recv()
        summed = part[tensor].astype(F32)
        for i in range(len(copies)):
            summed = summed + recv[i].astype(F32)
        out[...] = summed.astype(BF16)

    strip = min(512, width)

    def strip_of(index):
        return pl.ds(pl.multiple_of(index * strip, strip), strip)

    pair_o.wait_recv()
    mine, theirs = merged(y)
    outputs = unstack(
        (o_acc[y] * mine + o_recv[...].astype(F32) * theirs).T.astype(BF16)
    )

    @pl.loop(0, width // strip)
    def _(index):
        at = strip_of(index)
        term = matmul(outputs, wo[:, at], 1, 0).astype(BF16)
        for peer in range(tensors):
            part_out[peer, :, at] = term[peer * share : (peer + 1) * share]

    out_copies = share_out(part_out, recv_out, out_send, out_recv)
    next(scatter)
    pair_dq.wait_recv()
    query_pre = unstack(
        rot(
            (dq_acc[y] + dq_recv[...].astype(F32)).T * scale, spread(cosines), -spread(sines)
        ).astype(BF16)
    )

    @pl.loop(0, width // strip)
    def _(index):
        at = strip_of(index)
        acc_in[:, at] = matmul(query_pre, wq[at, :], 1, 1)

    next(scatter)
    add_up(part_out, recv_out, out_copies, attn_ref)
    next(scatter)
    key_pre = rot(k_sum[...], cosines, -sines).astype(BF16)
    value_sum = v_sum[...]
    value_pre = (mix_here * value_sum).astype(BF16)
    pre_own[...] = jnp.concatenate([key_pre, value_pre], axis=1)
    row_pre = []
    for step in (2, 1, 3):
        row_pre.append(
            send.go(
                send.build(
                    pre_own, pre_far.at[step - 1], row_send.at[2 + step], row_recv.at[2 + step],
                    "context", rank_of(y, turn(x, step, NX), z),
                )
            )
        )
    gfirst_ref[...] = (mix_first * value_sum).astype(BF16)

    @pl.loop(0, width // strip)
    def _(index):
        at = strip_of(index)
        term = (acc_in[:, at] + matmul(pre_own[...], wkv[at, :], 1, 1)).astype(BF16)
        for peer in range(tensors):
            part_in[peer, :, at] = term[peer * share : (peer + 1) * share]

    in_copies = share_out(part_in, recv_in, in_send, in_recv)
    many, rows = w_part.shape[1], w_part.shape[2]

    def term_of(side, pre):
        return matmul(side.reshape(NY * many * rows, length), pre, 1, 0)

    for copy in row_x + row_pre:
        copy.wait_recv()
    summed = term_of(xt[:, x], pre_own[...])
    for i in range(NX - 1):
        summed = summed + term_of(xt_far[i], pre_far[i])
    w_part[...] = summed.astype(BF16).reshape(w_part.shape)
    ring = []
    for step in (4, 3, 5, 2, 6, 1, 7):
        goal = turn(z, step, NZ)
        ring.append(
            send.go(
                send.build(
                    w_part.at[:, goal], w_far.at[step - 1], ring_send.at[step - 1],
                    ring_recv.at[step - 1], "context", rank_of(y, x, goal),
                )
            )
        )
    add_up(part_in, recv_in, in_copies, gin_ref)
    for copy in ring:
        copy.wait_recv()

    def strip_sum(half):
        total = w_part[half, z].astype(F32)
        for i in range(NZ - 1):
            total = total + w_far[i, half].astype(F32)
        return total

    w_low[...] = strip_sum(1 - y).astype(BF16)
    pair_w = send.go(
        send.build(
            w_low, w_last, pair_send.at[5], pair_recv.at[5], "context", rank_of(1 - y, x, z)
        )
    )
    weight = strip_sum(y)
    pair_w.wait_recv()
    weight = weight + w_last[...].astype(F32)
    gwk_ref[...] = weight[:, :HD]
    gwv_ref[...] = weight[:, HD:]
    send.finish()


def store_kernel(*refs):
    count = len(refs) // 2
    for i in range(count):
        refs[count + i][...] = refs[i][...]


def rope_tables(positions, head_width):
    half_width = head_width // 2
    exponent = jnp.arange(half_width, dtype=F32) * (2.0 / head_width)
    frequency = jnp.power(jnp.float32(THETA), -exponent)
    angles = positions.astype(F32)[:, None] * frequency[None, :]
    return (jnp.cos(angles), jnp.sin(angles))


def shards(hidden_in, value_first, w_query, w_key, w_value, w_out, value_mix, grad_out):
    tensors = lax.axis_size("tensor")
    length, width = hidden_in.shape[1:]
    features = w_query.shape[1]
    columns = features // HD * length
    share = length // tensors
    rows = width // (NY * NX * NZ)
    block_rows = lax.axis_index("context") * length + jnp.arange(length, dtype=jnp.int32)
    cosines, sines = rope_tables(block_rows, HD)
    tables = jnp.concatenate(
        [
            jnp.concatenate([cosines, cosines], axis=1),
            jnp.concatenate([-sines, sines], axis=1),
            jnp.broadcast_to(value_mix[:, :1], (2, HD)),
            jnp.zeros((6, HD), F32),
        ],
        axis=0,
    )
    vmem = pl.BlockSpec(memory_space=pltpu.VMEM)
    hbm = pl.BlockSpec(memory_space=pl.ANY)
    dma = pltpu.SemaphoreType.DMA

    def low(*shape):
        return pltpu.VMEM(shape, BF16)

    def full(*shape):
        return pltpu.VMEM(shape, F32)

    def fold_room(ends, count):
        return (
            low(4, 4, NX, count, HD), low(NY, ends, count, HD), low(NY, ends, 2, count, HD),
            low(4, 4, count, HD), low(NX, NY, count, HD), low(NY, ends, count, HD),
            low(3, NY, count, HD), low(2, NY, count, HD), low(2, count, HD),
        )

    others = (max(tensors - 1, 1),)
    scratch = [
        low(length, width), low(width, features), low(width, 2 * HD),
        low(features, width), low(length, width), low(NY, NX, NZ * rows, length), low(length, HD),
        low(length, HD), low(NY, NX, NH, length, HD), low(NY, NX, NH, length, HD),
        low(2, columns, HD), low(2, HD, columns), low(3 * NX, NH * length, columns),
        full(2, HD, columns), full(2, HD, columns), low(HD, columns), low(HD, columns),
        low(HD, columns), low(HD, columns), full(2, 8, columns), full(2, 8, columns),
        low(NY, NX, NH, length, HD), low(NY, NX, NH, length, HD), full(length, HD),
        full(length, HD), low(tensors, share, width), low(others[0], share, width),
        low(tensors, share, width), low(others[0], share, width), full(length, width),
        low(NX - 1, NY, NZ * rows, length), low(length, 2 * HD), low(NX - 1, length, 2 * HD),
        low(NY, NZ, rows, 2 * HD), low(NZ - 1, NY, rows, 2 * HD), low(rows, 2 * HD),
        low(rows, 2 * HD),
        fold_room(NH, length), dma((6,)),
        (dma((2,)), dma((2,)), dma((3,)), dma((3,)), dma((4, 4)), dma((4, 4)), dma((4, 4, NX)),
         dma((4, 4, NX)), dma((NY, NH, 2)), dma((NY, NH, 2)), dma((NY, NH)), dma((NY, NH))),
    ]

    def fold_sems(ends):
        return (
            dma((4, 4, NX)), dma((4, 4, NX)), dma((NY, ends)), dma((NY, ends)),
            dma((NY, ends, 2)), dma((NY, ends, 2)), dma((4, 4)), dma((4, 4)), dma((3,)), dma((3,)),
            dma((2,)), dma((2,)),
        )

    scratch += [fold_sems(NH), dma((6,)), dma((6,)), dma((NZ - 1,)), dma((NZ - 1,))]
    scratch += [dma((6,)), dma((6,))] + [dma(others)] * 6
    results = pl.pallas_call(
        block_kernel,
        out_shape=(
            jax.ShapeDtypeStruct((share, width), BF16),
            jax.ShapeDtypeStruct((share, width), BF16),
            jax.ShapeDtypeStruct((length, HD), BF16),
            jax.ShapeDtypeStruct((rows, HD), F32),
            jax.ShapeDtypeStruct((rows, HD), F32),
        ),
        in_specs=[hbm, vmem, hbm, hbm, hbm, hbm, hbm, vmem],
        out_specs=(vmem,) * 5,
        scratch_shapes=scratch,
        compiler_params=pltpu.CompilerParams(
            collective_id=1, has_side_effects=True, vmem_limit_bytes=56 * 2**20
        ),
        name="attention_block",
    )(
        hidden_in.reshape(length, width), value_first.reshape(length, HD), w_query, w_key, w_value,
        w_out, grad_out.reshape(share, width), tables,
    )
    attn_out, grad_in, grad_first, key_weight, value_weight = pl.pallas_call(
        store_kernel,
        out_shape=tuple(jax.ShapeDtypeStruct(part.shape, part.dtype) for part in results),
        in_specs=[vmem] * len(results),
        out_specs=(vmem,) * len(results),
        name="store_results",
    )(*results)
    return (
        attn_out.reshape(1, share, width),
        grad_in.reshape(1, share, width),
        grad_first.reshape(1, length, HD),
        key_weight,
        value_weight,
    )


def solution(mesh):
    return jax.shard_map(
        shards,
        mesh=mesh,
        in_specs=(
            P("context", None, None),
            P("context", None, "tensor"),
            P(None, "tensor"),
            P(None, "tensor"),
            P(None, "tensor"),
            P("tensor", None),
            P(None, "tensor"),
            P("context", "tensor", None),
        ),
        out_specs=(
            P("context", "tensor", None),
            P("context", "tensor", None),
            P("context", None, "tensor"),
            P("context", "tensor"),
            P("context", "tensor"),
        ),
        check_vma=False,
    )
```

time: 144 us -> 117 us (0.81)
  Pallas kernels: 131 us -> 113 us
  local copies, waits for them, and re-layouts: 8.76 us -> 0.74 us
    pallas_call x1, Pallas kernels: 131 us -> 111 us  [shards(): pl.pallas_call(block_kernel, out_shape=(jax.ShapeDtypeStruct((share, widt...]
    unnamed x6 -> x0, local copies, waits for them, and re-layouts: 8.76 us -> none
    pallas_call x0 -> x1, Pallas kernels: none -> 1.88 us  [shards(): pl.pallas_call(store_kernel, out_shape=tuple((jax.ShapeDtypeStruct(part.s...]
where the time goes in v3:
time: 117 us; the launch traced here: 116 us
  Pallas kernels  113 us (97%)
    pallas_call x1, Pallas kernels, shards(): pl.pallas_call(block_kernel, out_shape=(jax.ShapeDtypeStruct((share, widt...  111 us

profile of v3, /device:TPU:32, one launch (start us, length us, event | category | flops | bytes accessed | tf_op | source)
XLA Modules:
  0.0 115.9 jit_solution(10935459448066565326)
XLA Ops:
  0.7 0.1 pad.5.clone
  0.7 0.7 pad.4.clone
  1.4 0.3 multiply_cosine_fusion
  1.7 0.8 maximum_maximum_fusion.table_ref
  2.6 111.5 %attention_block.1 = (bf16[32,4096]{1,0:T(8,128)(2,1)}, bf16[32,4096]{1,0:T(8,128)(2,1)}, bf16[128,128]{1,0:T(8,128)(2,1)}, f32[64,128]{1,0:T(8,128)}, f32[64,128]{1,0:T(8,128)}) custom-call(bf16[128,4096]{1,0:T(8,128)(2,1)} %bitcast.7, bf16[128,128]{1,0:T(8,128)(2,1)} %bitcast.9, bf16[4096,512]{1,0:T(8,128)(2,1)} %wq_hbm.1, bf16[4096,128]{1,0:T(8,128)(2,1)} %wk_hbm.1, ...), custom_call_target="tpu_custom_call" | custom-call | tf_op jit(solution)/shard_map/attention_block/pallas_call | solution.py:911
  114.0 1.9 %store_results.1 = (bf16[32,4096]{1,0:T(8,128)(2,1)}, bf16[32,4096]{1,0:T(8,128)(2,1)}, bf16[128,128]{1,0:T(8,128)(2,1)}, f32[64,128]{1,0:T(8,128)}, f32[64,128]{1,0:T(8,128)}) custom-call(bf16[32,4096]{1,0:T(8,128)(2,1)} %get-tuple-element.15.refs_0_, bf16[32,4096]{1,0:T(8,128)(2,1)} %get-tuple-element.16.refs_1_, ...), custom_call_target="tpu_custom_call" | custom-call | tf_op jit(solution)/shard_map/store_results/pallas_call | solution.py:931
  (3 shorter events, 0.0 us)

commit v4 on v3

--- a/solution.py
+++ b/solution.py
@@ -67,13 +67,37 @@
             when(condition, copy.wait_send)
 
 
+class Place:
+    def __init__(self):
+        rank = lax.axis_index("context")
+        self.rank = rank
+        self.y, self.x, self.z = rank // (NX * NZ), (rank // NZ) % NX, rank % NZ
+        self.z_ring = [lax.rem(self.z + step, NZ) for step in range(NZ)]
+        self.x_ring = [lax.rem(self.x + step, NX) for step in range(NX)]
+        self.halves = [at // 2 for at in self.z_ring]
+        even = lax.rem(self.z + self.y, 2) == 0
+        self.parity = (even, jnp.logical_not(even))
+
+    def z_at(self, step):
+        return self.z_ring[step % NZ]
+
+    def x_at(self, step):
+        return self.x_ring[step % NX]
+
+    def half(self, step):
+        return self.halves[step % NZ]
+
+    def holds(self, step):
+        return self.parity[step % 2]
+
+
 def gather_steps(send, place, k_own, v_own, k_all, v_all, sems):
-    y, x, z, holder = place
+    y, x, z = place.y, place.x, place.z
     y_send, y_recv, kx_send, kx_recv, vz_send, vz_recv, kz_send, kz_recv = sems[:8]
     vx_send, vx_recv, vf_send, vf_recv = sems[8:]
-    slot = z // 2
+    slot = place.half(0)
     partner = rank_of(1 - y, x, z)
-    lends = jnp.logical_not(holder(z))
+    lends = place.holds(1)
     pairs = [
         send.build(own, whole.at[y, x, slot], y_send.at[i], y_recv.at[i], "context", partner)
         for i, (own, whole) in enumerate(((k_own, k_all), (v_own, v_all)))
@@ -88,7 +112,7 @@
         v_all[y, x, slot] = v_own[...]
 
     pl.when(lends)(lend)
-    pl.when(holder(z))(keep)
+    pl.when(place.holds(0))(keep)
     send.started += [(lends, copy) for copy in pairs]
 
     kx = {}
@@ -96,24 +120,24 @@
         part = k_all.at[:, x, slot]
         kx[step] = send.build(
             part, part, kx_send.at[step - 1], kx_recv.at[step - 1], "context",
-            rank_of(y, turn(x, step, NX), z),
+            rank_of(y, place.x_at(step), z),
         )
     rows = (0, 1, 3, 2)
 
     def kz_copy(chain, hop, part_at):
         way, half, _, _ = CHAINS[chain]
-        part = k_all.at[half, turn(x, rows[part_at], NX), turn(z, -way * hop, NZ) // 2]
+        part = k_all.at[half, place.x_at(rows[part_at]), place.half(-way * hop)]
         return send.build(
             part, part, kz_send.at[chain, hop, part_at], kz_recv.at[chain, hop, part_at],
-            "context", rank_of(y, x, turn(z, way, NZ)),
+            "context", rank_of(y, x, place.z_at(way)),
         )
 
     def kz(hop, part_at):
         if hop == 0 and part_at:
-            pl.when(holder(z))(kx[NX - rows[part_at]].wait_recv)
+            pl.when(place.holds(0))(kx[NX - rows[part_at]].wait_recv)
         for chain in ORDER:
             if hop < CHAINS[chain][2]:
-                condition = holder(turn(z, -CHAINS[chain][0] * hop, NZ))
+                condition = place.holds(-CHAINS[chain][0] * hop)
                 copy = kz_copy(chain, hop, part_at)
 
                 def act():
@@ -126,10 +150,10 @@
 
     def vz_copy(chain, hop):
         way, half, _, _ = CHAINS[chain]
-        part = v_all.at[half, x, turn(z, -way * hop, NZ) // 2]
+        part = v_all.at[half, x, place.half(-way * hop)]
         return send.build(
             part, part, vz_send.at[chain, hop], vz_recv.at[chain, hop], "context",
-            rank_of(y, x, turn(z, way, NZ)),
+            rank_of(y, x, place.z_at(way)),
         )
 
     def vx_copy(half, at, way):
@@ -137,26 +161,26 @@
         side = 0 if way > 0 else 1
         return send.build(
             part, part, vx_send.at[half, at, side], vx_recv.at[half, at, side], "context",
-            rank_of(y, turn(x, way, NX), z),
+            rank_of(y, place.x_at(way), z),
         )
 
     def vf_copy(half, at):
         way = 1 if half == 0 else -1
-        part = v_all.at[half, turn(x, -way, NX), at]
+        part = v_all.at[half, place.x_at(-way), at]
         return send.build(
             part, part, vf_send.at[half, at], vf_recv.at[half, at], "context",
-            rank_of(y, turn(x, way, NX), z),
+            rank_of(y, place.x_at(way), z),
         )
 
     def pieces(distance):
         if distance == 0:
-            return [(None, holder(z), half, slot) for half in range(NY)]
+            return [(None, place.holds(0), half, slot) for half in range(NY)]
         found = []
         for chain in ORDER:
             way, half, hops, _ = CHAINS[chain]
             if distance <= hops:
-                origin = turn(z, -way * distance, NZ)
-                found.append((chain, holder(origin), half, origin // 2))
+                step = -way * distance
+                found.append((chain, place.holds(step), half, place.half(step)))
         return found
 
     def v_round(distance):
@@ -198,7 +222,7 @@
                 when(condition, act)
         for chain in ORDER:
             way, _, hops, _ = CHAINS[chain]
-            condition = holder(turn(z, -way * hops, NZ))
+            condition = place.holds(-way * hops)
 
             def act():
                 for part_at in range(NX):
@@ -214,8 +238,8 @@
         for copy in kx.values():
             copy.start()
 
-    pl.when(holder(z))(start_rows)
-    send.started += [(holder(z), copy) for copy in kx.values()]
+    pl.when(place.holds(0))(start_rows)
+    send.started += [(place.holds(0), copy) for copy in kx.values()]
     v_round(0)
     kz(0, 0)
     v_round(1)
@@ -249,28 +273,22 @@
     yield
 
 
-def fold_steps(send, place, parity, a_in, b_in, a_out, b_out, bufs, sems):
-    y, x, z, holder_of = place
-
-    def holder(at):
-        return holder_of(at) if parity else True
-
-    def index(at):
-        return at // 2 if parity else at
+def fold_steps(send, place, idle, a_in, b_in, a_out, b_out, bufs, sems):
+    y, x, z = place.y, place.x, place.z
 
     az_buf, far_buf, near_buf, bz_buf, a_sum, b_sum, ax_buf, low, y_buf = bufs
     az_send, az_recv, far_send, far_recv, near_send, near_recv, bz_send, bz_recv = sems[:8]
     ax_send, ax_recv, y_send, y_recv = sems[8:]
-    slot = index(z)
+    slot = place.half(0)
     rows = (2, 1, 3, 0)
 
     def az_copy(chain, hop, part_at):
         way, half, hops, _ = CHAINS[chain]
-        own = a_in.at[half, turn(x, rows[part_at], NX), index(turn(z, way * (hops - hop), NZ))]
+        own = a_in.at[half, place.x_at(rows[part_at]), place.half(way * (hops - hop))]
         source = az_buf.at[chain, hop - 1, part_at] if hop else own
         copy = send.build(
             source, az_buf.at[chain, hop, part_at], az_send.at[chain, hop, part_at],
-            az_recv.at[chain, hop, part_at], "context", rank_of(y, x, turn(z, way, NZ)),
+            az_recv.at[chain, hop, part_at], "context", rank_of(y, x, place.z_at(way)),
         )
         return own, copy
 
@@ -278,7 +296,7 @@
         for chain in ORDER:
             way, _, hops, _ = CHAINS[chain]
             if hop < hops:
-                condition = holder(turn(z, way * (hops - hop), NZ))
+                condition = place.holds(way * (hops - hop))
                 own, copy = az_copy(chain, hop, part_at)
 
                 def act():
@@ -291,14 +309,14 @@
                 send.started.append((condition, copy))
 
     def ax_copy(step):
-        goal = turn(x, step, NX)
+        goal = place.x_at(step)
         return send.build(
             a_sum.at[goal], ax_buf.at[step - 1], ax_send.at[step - 1], ax_recv.at[step - 1],
             "context", rank_of(y, goal, z),
         )
 
     def a_end(part_at):
-        row = turn(x, rows[part_at], NX)
+        row = place.x_at(rows[part_at])
 
         def act():
             for half in range(NY):
@@ -311,19 +329,19 @@
             if rows[part_at]:
                 ax_copy(rows[part_at]).start()
 
-        when(holder(z), act)
+        when(place.holds(0), act)
         if rows[part_at]:
-            send.started.append((holder(z), ax_copy(rows[part_at])))
+            send.started.append((place.holds(0), ax_copy(rows[part_at])))
 
     def pieces(distance):
         if distance == 0:
-            return [(None, holder(z), half, slot) for half in range(NY)]
+            return [(None, place.holds(0), half, slot) for half in range(NY)]
         found = []
         for chain in ORDER:
             way, half, hops, _ = CHAINS[chain]
             if distance <= hops:
-                goal = turn(z, way * distance, NZ)
-                found.append((chain, holder(goal), half, index(goal)))
+                step = way * distance
+                found.append((chain, place.holds(step), half, place.half(step)))
         return found
 
     def outward(half):
@@ -332,13 +350,13 @@
     def far_copy(half, at):
         way = outward(half)
         return send.build(
-            b_in.at[half, turn(x, 2, NX), at], far_buf.at[half, at], far_send.at[half, at],
-            far_recv.at[half, at], "context", rank_of(y, turn(x, way, NX), z),
+            b_in.at[half, place.x_at(2), at], far_buf.at[half, at], far_send.at[half, at],
+            far_recv.at[half, at], "context", rank_of(y, place.x_at(way), z),
         )
 
     def near_copy(half, at, way):
         side = 0 if way > 0 else 1
-        goal = turn(x, way, NX)
+        goal = place.x_at(way)
         source = far_buf.at[half, at] if way == outward(half) else b_in.at[half, goal, at]
         return send.build(
             source, near_buf.at[half, at, side], near_send.at[half, at, side],
@@ -362,7 +380,7 @@
 
             def act():
                 far_copy(half, at).wait_recv()
-                add_into(far_buf.at[half, at], b_in.at[half, turn(x, outward(half), NX), at])
+                add_into(far_buf.at[half, at], b_in.at[half, place.x_at(outward(half)), at])
                 copy.start()
 
             when(condition, act)
@@ -370,10 +388,10 @@
 
     def bz_copy(chain, hop):
         way, half, hops, _ = CHAINS[chain]
-        own = b_sum.at[half, index(turn(z, way * (hops - hop), NZ))]
+        own = b_sum.at[half, place.half(way * (hops - hop))]
         return send.build(
             own, bz_buf.at[chain, hop], bz_send.at[chain, hop], bz_recv.at[chain, hop],
-            "context", rank_of(y, x, turn(z, way, NZ)),
+            "context", rank_of(y, x, place.z_at(way)),
         )
 
     def b_end(distance):
@@ -412,8 +430,8 @@
     ]
 
     def hand_over(i):
-        when(holder(z), pairs[i].start)
-        send.started.append((holder(z), pairs[i]))
+        when(place.holds(0), pairs[i].start)
+        send.started.append((place.holds(0), pairs[i]))
 
     def close(i, out):
         def keep():
@@ -423,12 +441,8 @@
             pairs[i].wait_recv()
             out[...] = y_buf[i].astype(F32)
 
-        if parity:
-            pl.when(holder(z))(keep)
-            pl.when(jnp.logical_not(holder(z)))(take)
-        else:
-            pairs[i].wait_recv()
-            out[...] = low[i, y].astype(F32) + y_buf[i].astype(F32)
+        pl.when(place.holds(0))(keep)
+        pl.when(place.holds(1))(take)
 
     def a_row():
         for step in (1, 2, 3):
@@ -448,36 +462,18 @@
     az(0, 3)
     b_start(0)
     yield
-    b_middle(4)
-    b_middle(3)
-    az(1, 0)
-    az(1, 1)
-    b_middle(2)
-    b_end(4)
-    b_end(3)
-    yield
-    az(1, 2)
-    az(2, 0)
-    b_middle(1)
-    az(1, 3)
-    az(2, 1)
-    b_middle(0)
-    b_end(2)
-    az(3, 0)
-    az(2, 2)
-    az(3, 1)
-    b_end(1)
-    a_end(0)
-    yield
-    az(2, 3)
-    az(3, 2)
-    a_end(1)
-    az(3, 3)
-    a_end(2)
-    b_end(0)
+    for work, arguments in (
+        (b_middle, (4,)), (b_middle, (3,)), (az, (1, 0)), (az, (1, 1)), (b_middle, (2,)),
+        (b_end, (4,)), (b_end, (3,)), (az, (1, 2)), (az, (2, 0)), (b_middle, (1,)), (az, (1, 3)),
+        (az, (2, 1)), (b_middle, (0,)), (b_end, (2,)), (az, (3, 0)), (az, (2, 2)), (az, (3, 1)),
+        (b_end, (1,)), (a_end, (0,)), (az, (2, 3)), (az, (3, 2)), (a_end, (1,)), (az, (3, 3)),
+        (a_end, (2,)), (b_end, (0,)),
+    ):
+        work(*arguments)
+        idle()
     hand_over(1)
     a_end(3)
-    when(holder(z), a_row)
+    when(place.holds(0), a_row)
     hand_over(0)
     close(1, b_out)
     close(0, a_out)
@@ -489,13 +485,13 @@
     attn_ref, gin_ref, gfirst_ref, gwk_ref, gwv_ref,
     x_buf, wq, wkv, wo, g_all, xt, k_own, v_own, k_all, v_all, q_all, cot_all, weights,
     o_acc, dq_acc, o_send, o_recv, dq_send, dq_recv, stat_mine, stat_pair, dk_all, dv_all,
-    k_sum, v_sum, part_out, recv_out, part_in, recv_in, acc_in, xt_far,
+    k_sum, v_sum, part_out, recv_out, part_in, recv_in, xt_far,
     pre_own, pre_far, w_part, w_far, w_low, w_last, grad_bufs, local_sem, gather_sems, grad_sems,
     row_send, row_recv, ring_send, ring_recv,
     pair_send, pair_recv, g_send, g_recv, out_send, out_recv, in_send, in_recv,
 ):
-    rank = lax.axis_index("context")
-    y, x, z = rank // (NX * NZ), (rank // NZ) % NX, rank % NZ
+    place = Place()
+    y, x, z = place.y, place.x, place.z
     tensor, tensors = lax.axis_index("tensor"), lax.axis_size("tensor")
     length, width = x_buf.shape
     columns = q_all.shape[1]
@@ -505,10 +501,6 @@
     scale = HD ** (-0.5)
     factor = scale * LOG2E
 
-    def holder(at):
-        return lax.rem(at + y, 2) == 0
-
-    place = (y, x, z, holder)
     other = rank_of(1 - y, NX - 1 - x, z)
     peers = [lax.rem(tensor + step, tensors) for step in range(1, tensors)]
     my_rows = pl.ds(pl.multiple_of(tensor * share, share), share)
@@ -584,10 +576,9 @@
     for copy in g_copies:
         copy.wait_recv()
     loads[5].wait()
+    cotangent = matmul(wo[...], g_all[...], 1, 1).astype(BF16)
     for h in range(heads):
-        cot_all[y, :, h * length : (h + 1) * length] = matmul(
-            wo[h * HD : (h + 1) * HD, :], g_all[...], 1, 1
-        ).astype(BF16)
+        cot_all[y, :, h * length : (h + 1) * length] = cotangent[h * HD : (h + 1) * HD]
     pair_cot = send.go(
         send.build(cot_all.at[y], cot_all.at[y], pair_send.at[1], pair_recv.at[1], "context", other)
     )
@@ -699,15 +690,6 @@
             0, row_of(slot) + 1, back, jnp.zeros((HD, columns), F32)
         )
 
-    scatter = fold_steps(
-        send, place, True, dk_all, dv_all, k_sum, v_sum, grad_bufs, grad_sems
-    )
-    next(scatter)
-    dq_send[...] = dq_acc[1 - y].astype(BF16)
-    pair_dq = send.go(
-        send.build(dq_send, dq_recv, pair_send.at[4], pair_recv.at[4], "context", other)
-    )
-
     def share_out(part, recv, send_sem, recv_sem):
         return [
             send.go(
@@ -727,40 +709,35 @@
         out[...] = summed.astype(BF16)
 
     strip = min(512, width)
-
-    def strip_of(index):
-        return pl.ds(pl.multiple_of(index * strip, strip), strip)
-
-    pair_o.wait_recv()
-    mine, theirs = merged(y)
-    outputs = unstack(
-        (o_acc[y] * mine + o_recv[...].astype(F32) * theirs).T.astype(BF16)
-    )
-
-    @pl.loop(0, width // strip)
-    def _(index):
-        at = strip_of(index)
-        term = matmul(outputs, wo[:, at], 1, 0).astype(BF16)
-        for peer in range(tensors):
-            part_out[peer, :, at] = term[peer * share : (peer + 1) * share]
-
-    out_copies = share_out(part_out, recv_out, out_send, out_recv)
-    next(scatter)
-    pair_dq.wait_recv()
-    query_pre = unstack(
-        rot(
-            (dq_acc[y] + dq_recv[...].astype(F32)).T * scale, spread(cosines), -spread(sines)
-        ).astype(BF16)
-    )
-
-    @pl.loop(0, width // strip)
-    def _(index):
-        at = strip_of(index)
-        acc_in[:, at] = matmul(query_pre, wq[at, :], 1, 1)
-
-    next(scatter)
-    add_up(part_out, recv_out, out_copies, attn_ref)
-    next(scatter)
+    strips = [slice(at, at + strip) for at in range(0, width, strip)]
+
+    def other_work():
+        pair_o.wait_recv()
+        mine, theirs = merged(y)
+        outputs = unstack(
+            (o_acc[y] * mine + o_recv[...].astype(F32) * theirs).T.astype(BF16)
+        )
+        for at in strips:
+            term = matmul(outputs, wo[:, at], 1, 0).astype(BF16)
+            for peer in range(tensors):
+                part_out[peer, :, at] = term[peer * share : (peer + 1) * share]
+            yield
+        out_copies.extend(share_out(part_out, recv_out, out_send, out_recv))
+        yield
+
+    out_copies = []
+    work = other_work()
+    fold = fold_steps(
+        send, place, lambda: next(work, None), dk_all, dv_all, k_sum, v_sum, grad_bufs, grad_sems
+    )
+    next(fold)
+    dq_send[...] = dq_acc[1 - y].astype(BF16)
+    pair_dq = send.go(
+        send.build(dq_send, dq_recv, pair_send.at[4], pair_recv.at[4], "context", other)
+    )
+    next(fold)
+    for _ in work:
+        pass
     key_pre = rot(k_sum[...], cosines, -sines).astype(BF16)
     value_sum = v_sum[...]
     value_pre = (mix_here * value_sum).astype(BF16)
@@ -777,10 +754,15 @@
         )
     gfirst_ref[...] = (mix_first * value_sum).astype(BF16)
 
-    @pl.loop(0, width // strip)
-    def _(index):
-        at = strip_of(index)
-        term = (acc_in[:, at] + matmul(pre_own[...], wkv[at, :], 1, 1)).astype(BF16)
+    pair_dq.wait_recv()
+    query_pre = unstack(
+        rot(
+            (dq_acc[y] + dq_recv[...].astype(F32)).T * scale, spread(cosines), -spread(sines)
+        ).astype(BF16)
+    )
+    for at in strips:
+        term = matmul(query_pre, wq[at, :], 1, 1) + matmul(pre_own[...], wkv[at, :], 1, 1)
+        term = term.astype(BF16)
         for peer in range(tensors):
             part_in[peer, :, at] = term[peer * share : (peer + 1) * share]
 
@@ -796,6 +778,8 @@
     for i in range(NX - 1):
         summed = summed + term_of(xt_far[i], pre_far[i])
     w_part[...] = summed.astype(BF16).reshape(w_part.shape)
+    earlier = Sender()
+    earlier.started, send.started = send.started, []
     ring = []
     for step in (4, 3, 5, 2, 6, 1, 7):
         goal = turn(z, step, NZ)
@@ -807,6 +791,8 @@
                 )
             )
         )
+    add_up(part_out, recv_out, out_copies, attn_ref)
+    earlier.finish()
     add_up(part_in, recv_in, in_copies, gin_ref)
     for copy in ring:
         copy.wait_recv()
@@ -890,7 +876,7 @@
         low(HD, columns), low(HD, columns), full(2, 8, columns), full(2, 8, columns),
         low(NY, NX, NH, length, HD), low(NY, NX, NH, length, HD), full(length, HD),
         full(length, HD), low(tensors, share, width), low(others[0], share, width),
-        low(tensors, share, width), low(others[0], share, width), full(length, width),
+        low(tensors, share, width), low(others[0], share, width),
         low(NX - 1, NY, NZ * rows, length), low(length, 2 * HD), low(NX - 1, length, 2 * HD),
         low(NY, NZ, rows, 2 * HD), low(NZ - 1, NY, rows, 2 * HD), low(rows, 2 * HD),
         low(rows, 2 * HD),

time: 117 us -> 115 us (0.983)
  no operation moved by 1% of the time
where the time goes in v4:
time: 115 us
  Pallas kernels  112 us (97%)
    pallas_call x1, Pallas kernels, shards(): pl.pallas_call(block_kernel, out_shape=(jax.ShapeDtypeStruct((share, widt...  110 us

profile of v4, /device:TPU:32, one launch (start us, length us, event | category | flops | bytes accessed | tf_op | source)
XLA Modules:
  0.0 114.9 jit_solution(3968502658683077465)
XLA Ops:
  0.7 0.1 pad.5.clone
  0.7 0.7 pad.4.clone
  1.4 0.3 multiply_cosine_fusion
  1.7 0.8 maximum_maximum_fusion.table_ref
  2.6 110.4 %attention_block.1 = (bf16[32,4096]{1,0:T(8,128)(2,1)}, bf16[32,4096]{1,0:T(8,128)(2,1)}, bf16[128,128]{1,0:T(8,128)(2,1)}, f32[64,128]{1,0:T(8,128)}, f32[64,128]{1,0:T(8,128)}) custom-call(bf16[128,4096]{1,0:T(8,128)(2,1)} %bitcast.7, bf16[128,128]{1,0:T(8,128)(2,1)} %bitcast.9, bf16[4096,512]{1,0:T(8,128)(2,1)} %wq_hbm.1, bf16[4096,128]{1,0:T(8,128)(2,1)} %wk_hbm.1, ...), custom_call_target="tpu_custom_call" | custom-call | tf_op jit(solution)/shard_map/attention_block/pallas_call | solution.py:897
  113.0 1.9 %store_results.1 = (bf16[32,4096]{1,0:T(8,128)(2,1)}, bf16[32,4096]{1,0:T(8,128)(2,1)}, bf16[128,128]{1,0:T(8,128)(2,1)}, f32[64,128]{1,0:T(8,128)}, f32[64,128]{1,0:T(8,128)}) custom-call(bf16[32,4096]{1,0:T(8,128)(2,1)} %get-tuple-element.15.refs_0_, bf16[32,4096]{1,0:T(8,128)(2,1)} %get-tuple-element.16.refs_1_, ...), custom_call_target="tpu_custom_call" | custom-call | tf_op jit(solution)/shard_map/store_results/pallas_call | solution.py:917
  (3 shorter events, 0.0 us)

commit v5 on v4

--- a/solution.py
+++ b/solution.py
@@ -512,7 +512,7 @@
              (wo_hbm, wo))
         )
     ]
-    for copy in loads:
+    for copy in loads[:5]:
         copy.start()
     barrier = pltpu.get_barrier_semaphore()
     ranks = [rank_of(1 - y, x, z), rank_of(y, x, turn(z, 1, NZ)), rank_of(y, x, turn(z, -1, NZ))]
@@ -545,6 +545,7 @@
 
     for copy in loads[:3]:
         copy.wait()
+    loads[5].start()
     projected = matmul(x_buf[...], wkv[...], 1, 0)
     k_own[...] = rot(projected[:, :HD], cosines, sines).astype(BF16)
     v_own[...] = (
@@ -606,8 +607,7 @@
     def tile_of(ref, row):
         return ref[row // NX, lax.rem(row, NX)].reshape(tile, HD)
 
-    @pl.loop(0, 2)
-    def _(slot):
+    def forward(slot):
         last = row_of(slot)
         visible = key_in_tile <= query_in_block + z * length
         queries = q_all[slot].astype(F32).T.astype(BF16)
@@ -641,21 +641,26 @@
         stat_mine[slot, 1:2] = totals
         o_acc[slot] = output
 
-    pair_cot.wait_recv()
-    for slot in range(2):
+    pair_stat = {}
+    for slot in (1, 0):
+        forward(slot)
+        if slot == 1:
+            pair_cot.wait_recv()
         stat_mine[slot, 2:3] = jnp.sum(
             cot_all[slot].astype(F32) * o_acc[slot], axis=0, keepdims=True
         )
-    pair_stat = send.go(
-        send.build(stat_mine, stat_pair, pair_send.at[2], pair_recv.at[2], "context", other)
-    )
+        pair_stat[slot] = send.go(
+            send.build(
+                stat_mine.at[slot], stat_pair.at[slot], pair_send.at[5 + slot],
+                pair_recv.at[5 + slot], "context", other,
+            )
+        )
     o_send[...] = o_acc[1 - y].astype(BF16)
     pair_o = send.go(
         send.build(o_send, o_recv, pair_send.at[3], pair_recv.at[3], "context", other)
     )
     dk_all[...] = jnp.zeros(dk_all.shape, BF16)
     dv_all[...] = jnp.zeros(dv_all.shape, BF16)
-    pair_stat.wait_recv()
 
     def merged(slot):
         top = jnp.maximum(stat_mine[slot, 0:1], stat_pair[slot, 0:1])
@@ -664,9 +669,7 @@
         inverse = 1.0 / (stat_mine[slot, 1:2] * mine + stat_pair[slot, 1:2] * theirs)
         return mine * inverse, theirs * inverse
 
-    @pl.loop(0, 2)
-    def _(step):
-        slot = 1 - step
+    def backward(slot):
         mine, theirs = merged(slot)
         delta = (stat_mine[slot, 2:3] * mine + stat_pair[slot, 2:3] * theirs) * mine
         scaled = cot_all[slot].astype(F32) * mine
@@ -689,6 +692,10 @@
         dq_acc[slot] = lax.fori_loop(
             0, row_of(slot) + 1, back, jnp.zeros((HD, columns), F32)
         )
+
+    for slot in (1, 0):
+        pair_stat[slot].wait_recv()
+        backward(slot)
 
     def share_out(part, recv, send_sem, recv_sem):
         return [
@@ -806,7 +813,7 @@
     w_low[...] = strip_sum(1 - y).astype(BF16)
     pair_w = send.go(
         send.build(
-            w_low, w_last, pair_send.at[5], pair_recv.at[5], "context", rank_of(1 - y, x, z)
+            w_low, w_last, pair_send.at[2], pair_recv.at[2], "context", rank_of(1 - y, x, z)
         )
     )
     weight = strip_sum(y)
@@ -893,7 +900,7 @@
         )
 
     scratch += [fold_sems(NH), dma((6,)), dma((6,)), dma((NZ - 1,)), dma((NZ - 1,))]
-    scratch += [dma((6,)), dma((6,))] + [dma(others)] * 6
+    scratch += [dma((7,)), dma((7,))] + [dma(others)] * 6
     results = pl.pallas_call(
         block_kernel,
         out_shape=(

time: 115 us -> 114 us (level)
    pallas_call x1, Pallas kernels: 110 us -> 109 us  [shards(): pl.pallas_call(block_kernel, out_shape=(jax.ShapeDtypeStruct((share, widt...]
where the time goes in v5:
time: 114 us; the launch traced here: 113 us
  Pallas kernels  111 us (97%)
  other arithmetic  1.15 us (1%)
    pallas_call x1, Pallas kernels, shards(): pl.pallas_call(block_kernel, out_shape=(jax.ShapeDtypeStruct((share, widt...  109 us

profile of v5, /device:TPU:32, one launch (start us, length us, event | category | flops | bytes accessed | tf_op | source)
XLA Modules:
  0.0 113.5 jit_solution(12416712576099251138)
XLA Ops:
  0.7 0.1 pad.5.clone
  0.7 0.7 pad.4.clone
  1.4 0.3 multiply_cosine_fusion
  1.7 0.8 maximum_maximum_fusion.table_ref
  2.6 109.0 %attention_block.1 = (bf16[32,4096]{1,0:T(8,128)(2,1)}, bf16[32,4096]{1,0:T(8,128)(2,1)}, bf16[128,128]{1,0:T(8,128)(2,1)}, f32[64,128]{1,0:T(8,128)}, f32[64,128]{1,0:T(8,128)}) custom-call(bf16[128,4096]{1,0:T(8,128)(2,1)} %bitcast.7, bf16[128,128]{1,0:T(8,128)(2,1)} %bitcast.9, bf16[4096,512]{1,0:T(8,128)(2,1)} %wq_hbm.1, bf16[4096,128]{1,0:T(8,128)(2,1)} %wk_hbm.1, ...), custom_call_target="tpu_custom_call" | custom-call | tf_op jit(solution)/shard_map/attention_block/pallas_call | solution.py:904
  111.6 1.9 %store_results.1 = (bf16[32,4096]{1,0:T(8,128)(2,1)}, bf16[32,4096]{1,0:T(8,128)(2,1)}, bf16[128,128]{1,0:T(8,128)(2,1)}, f32[64,128]{1,0:T(8,128)}, f32[64,128]{1,0:T(8,128)}) custom-call(bf16[32,4096]{1,0:T(8,128)(2,1)} %get-tuple-element.15.refs_0_, bf16[32,4096]{1,0:T(8,128)(2,1)} %get-tuple-element.16.refs_1_, ...), custom_call_target="tpu_custom_call" | custom-call | tf_op jit(solution)/shard_map/store_results/pallas_call | solution.py:924
  (3 shorter events, 0.0 us)
